TPU v7x, 32 devices: a whole 2x2x4 slice. The times are simulated.
32 devices in a mesh: dp: 8 (over z, y), fsdp: 4 (over x, core).
Axes of the slice: x: 2, y: 2, z: 4, core: 2. Of those that a mesh axis runs over, the one named last changes fastest.
Arguments:
- tokens: bfloat16 [65536, 512], P(('dp', 'fsdp')), may hold values from -6 to 6
- cotangent: bfloat16 [65536, 512], P(('dp', 'fsdp')), may hold values from -6 to 6
- cond_frames: int32 [64], P(('dp', 'fsdp')), may hold values from 1 to 3
- qkv_weight: float32 [32, 24576], P(('dp', 'fsdp')), may hold values from -0.25 to 0.25
- proj_weight: float32 [32, 8192], P(('dp', 'fsdp')), may hold values from -0.375 to 0.375
- up_weight: float32 [32, 32768], P(('dp', 'fsdp')), may hold values from -0.25 to 0.25
- down_weight: float32 [32, 32768], P(('dp', 'fsdp')), may hold values from -0.125 to 0.125
- vectors: float32 [32, 208], P(('dp', 'fsdp')), may hold values from -0.6 to 1.4, as said below
- qkv_first: float32 [32, 24576], P(('dp', 'fsdp')), may hold values from -160 to 160
- proj_first: float32 [32, 8192], P(('dp', 'fsdp')), may hold values from -40 to 40
- up_first: float32 [32, 32768], P(('dp', 'fsdp')), may hold values from -80 to 80
- down_first: float32 [32, 32768], P(('dp', 'fsdp')), may hold values from -80 to 80
- vector_first: float32 [32, 208], P(('dp', 'fsdp')), may hold values from -128 to 128
- qkv_second: float32 [32, 24576], P(('dp', 'fsdp')), may hold values from 1703.936 to 27525.12
- proj_second: float32 [32, 8192], P(('dp', 'fsdp')), may hold values from 163.84 to 655.36
- up_second: float32 [32, 32768], P(('dp', 'fsdp')), may hold values from 340.7872 to 5505.024
- down_second: float32 [32, 32768], P(('dp', 'fsdp')), may hold values from 340.7872 to 5505.024
- vector_second: float32 [32, 208], P(('dp', 'fsdp')), may hold values from 851.968 to 13762.56
- qkv_average: float32 [32, 24576], P(('dp', 'fsdp')), may hold values from -0.25 to 0.25
- proj_average: float32 [32, 8192], P(('dp', 'fsdp')), may hold values from -0.375 to 0.375
- up_average: float32 [32, 32768], P(('dp', 'fsdp')), may hold values from -0.25 to 0.25
- down_average: float32 [32, 32768], P(('dp', 'fsdp')), may hold values from -0.125 to 0.125
- vector_average: float32 [32, 208], P(('dp', 'fsdp')), may hold values from 0.5 to 1.5
Outputs:
- output: bfloat16 [65536, 512], P(('dp', 'fsdp'))
- input_grad: float32 [65536, 512], P(('dp', 'fsdp'))
- qkv_first_new: float32 [32, 24576], P(('dp', 'fsdp'))
- qkv_second_new: float32 [32, 24576], P(('dp', 'fsdp'))
- qkv_weight_new: float32 [32, 24576], P(('dp', 'fsdp'))
- qkv_average_new: float32 [32, 24576], P(('dp', 'fsdp'))
- proj_first_new: float32 [32, 8192], P(('dp', 'fsdp'))
- proj_second_new: float32 [32, 8192], P(('dp', 'fsdp'))
- proj_weight_new: float32 [32, 8192], P(('dp', 'fsdp'))
- proj_average_new: float32 [32, 8192], P(('dp', 'fsdp'))
- up_first_new: float32 [32, 32768], P(('dp', 'fsdp'))
- up_second_new: float32 [32, 32768], P(('dp', 'fsdp'))
- up_weight_new: float32 [32, 32768], P(('dp', 'fsdp'))
- up_average_new: float32 [32, 32768], P(('dp', 'fsdp'))
- down_first_new: float32 [32, 32768], P(('dp', 'fsdp'))
- down_second_new: float32 [32, 32768], P(('dp', 'fsdp'))
- down_weight_new: float32 [32, 32768], P(('dp', 'fsdp'))
- down_average_new: float32 [32, 32768], P(('dp', 'fsdp'))
- vector_first_new: float32 [32, 208], P(('dp', 'fsdp'))
- vector_second_new: float32 [32, 208], P(('dp', 'fsdp'))
- vector_new: float32 [32, 208], P(('dp', 'fsdp'))
- vector_average_new: float32 [32, 208], P(('dp', 'fsdp'))
Inputs may be any that keep to these rules, and one draw needn't show every extreme that they name: `cond_frames`: each clip's first frame is always conditioning. `vectors`: entries of g1 and g2 are gains, the others biases.
All inputs are finite; a program needn't handle non-finite values.
Results may differ from a plain program's by a relative error of at most 0.0093.
Values may be sent and summed in bfloat16 or wider, within the bound.
A program may use at most 192 MiB of HBM per device.

v0:
```python
import jax
import jax.numpy as jnp
from jax import lax
from jax.sharding import PartitionSpec as P

D = 512
FF = 2048
HEADS = 8
HEAD_DIM = 64
FRAME_TOK = 64
STEP = 10
CLIP_LEN = 1024


EPS = 1e-05
BETA_ONE = 0.9
BETA_TWO = 0.95
ADAM_EPS = 1e-08
RATE_MATRIX = 0.02
RATE_VECTOR = 0.2
WEIGHT_DECAY = 0.1
EMA_KEEP = 0.9
NEG = -1e30


def layer_norm(inputs, gain_vec, shifts):
    row_mean = jnp.mean(inputs, axis=-1, keepdims=True)
    centred = inputs - row_mean
    variance = jnp.mean(centred * centred, axis=-1, keepdims=True)
    return centred * lax.rsqrt(variance + EPS) * gain_vec + shifts


def split_vectors(packed):
    bounds = [0, D, 2 * D, 5 * D, 6 * D, 7 * D, 8 * D, 8 * D + FF, 9 * D + FF]
    return [packed[bounds[i] : bounds[i + 1]] for i in range(8)]


def unpack(gathered):
    qkv_mat = gathered[0].reshape(D, 3 * D)
    proj_mat = gathered[1].reshape(D, D)
    up_mat = gathered[2].reshape(D, FF)
    down_mat = gathered[3].reshape(FF, D)
    packed = gathered[4].reshape(-1).astype(jnp.float32)
    return (qkv_mat, proj_mat, up_mat, down_mat, packed)


def split_heads(qkv_clip):
    length = qkv_clip.shape[0]
    queries = qkv_clip[:, :D].reshape(length, HEADS, HEAD_DIM)
    keys_part = qkv_clip[:, D : 2 * D].reshape(length, HEADS, HEAD_DIM)
    values_part = qkv_clip[:, 2 * D :].reshape(length, HEADS, HEAD_DIM)
    return (queries, keys_part, values_part)


def block_scores(q_block, k_block, start):
    scores = jnp.einsum(
        "qhd,khd->hqk", q_block, k_block, preferred_element_type=jnp.float32
    ) * HEAD_DIM ** (-0.5)
    row_index = start + jnp.arange(q_block.shape[0])[:, None]
    col_index = jnp.arange(k_block.shape[0])[None, :]
    return jnp.where(col_index <= row_index, scores, NEG)


def attend_forward(qkv_clip):
    length = qkv_clip.shape[0]
    block = min(512, length)
    queries, keys_part, values_part = split_heads(qkv_clip)
    outs_list = []
    lse_list = []
    for start in range(0, length, block):
        stop = start + block
        scores = block_scores(queries[start:stop], keys_part[:stop], start)
        row_top = jnp.max(scores, axis=-1, keepdims=True)
        exponent = jnp.exp(scores - row_top)
        total = jnp.sum(exponent, axis=-1, keepdims=True)
        attn_probs = exponent / total
        outs_list.append(
            jnp.einsum(
                "hqk,khd->qhd",
                attn_probs.astype(jnp.bfloat16),
                values_part[:stop],
                preferred_element_type=jnp.float32,
            )
        )
        lse_list.append(row_top[..., 0] + jnp.log(total[..., 0]))
    return (
        jnp.concatenate(outs_list, axis=0).reshape(length, D),
        jnp.concatenate(lse_list, axis=1),
    )


def attend_backward(bundle):
    qkv_clip, grad_clip, lse_clip = bundle
    length = qkv_clip.shape[0]
    block = min(512, length)
    scale = HEAD_DIM ** (-0.5)
    queries, keys_part, values_part = split_heads(qkv_clip)
    grad_heads = grad_clip.reshape(length, HEADS, HEAD_DIM)
    grad_q_list = []
    grad_k = jnp.zeros((length, HEADS, HEAD_DIM), jnp.float32)
    grad_v = jnp.zeros((length, HEADS, HEAD_DIM), jnp.float32)
    for start in range(0, length, block):
        stop = start + block
        scores = block_scores(queries[start:stop], keys_part[:stop], start)
        attn_probs = jnp.exp(scores - lse_clip[:, start:stop, None])
        go_block = grad_heads[start:stop]
        grad_v = grad_v.at[:stop].add(
            jnp.einsum(
                "hqk,qhd->khd",
                attn_probs.astype(jnp.bfloat16),
                go_block,
                preferred_element_type=jnp.float32,
            )
        )
        grad_p = jnp.einsum(
            "qhd,khd->hqk", go_block, values_part[:stop], preferred_element_type=jnp.float32
        )
        row_dot = jnp.sum(grad_p * attn_probs, axis=-1, keepdims=True)
        grad_s = (attn_probs * (grad_p - row_dot)).astype(jnp.bfloat16)
        grad_q_list.append(
            jnp.einsum("hqk,khd->qhd", grad_s, keys_part[:stop], preferred_element_type=jnp.float32)
            * scale
        )
        grad_k = grad_k.at[:stop].add(
            jnp.einsum(
                "hqk,qhd->khd", grad_s, queries[start:stop], preferred_element_type=jnp.float32
            )
            * scale
        )
    grad_q = jnp.concatenate(grad_q_list, axis=0)
    return jnp.concatenate(
        [grad_q.reshape(length, D), grad_k.reshape(length, D), grad_v.reshape(length, D)], axis=1
    ).astype(jnp.bfloat16)


def adamw(weight, grad, first, second, average, rate, decay):
    first_new = BETA_ONE * first + (1.0 - BETA_ONE) * grad
    second_new = BETA_TWO * second + (1.0 - BETA_TWO) * grad * grad
    first_hat = first_new / (1.0 - BETA_ONE**STEP)
    second_hat = second_new / (1.0 - BETA_TWO**STEP)
    weight_new = weight - rate * (first_hat / (jnp.sqrt(second_hat) + ADAM_EPS) + decay * weight)
    average_new = EMA_KEEP * average + (1.0 - EMA_KEEP) * weight_new
    return (first_new, second_new, weight_new, average_new)


def local(
    tokens,
    cotangent,
    cond_frames,
    qkv_weight,
    proj_weight,
    up_weight,
    down_weight,
    vectors,
    qkv_first,
    proj_first,
    up_first,
    down_first,
    vector_first,
    qkv_second,
    proj_second,
    up_second,
    down_second,
    vector_second,
    qkv_average,
    proj_average,
    up_average,
    down_average,
    vector_average,
):
    shards = lax.axis_size(("dp", "fsdp"))
    gathered = (
        lax.all_gather(qkv_weight.astype(jnp.bfloat16), ("dp", "fsdp"), axis=0, tiled=True),
        lax.all_gather(proj_weight.astype(jnp.bfloat16), ("dp", "fsdp"), axis=0, tiled=True),
        lax.all_gather(up_weight.astype(jnp.bfloat16), ("dp", "fsdp"), axis=0, tiled=True),
        lax.all_gather(down_weight.astype(jnp.bfloat16), ("dp", "fsdp"), axis=0, tiled=True),
        lax.all_gather(vectors.astype(jnp.bfloat16), ("dp", "fsdp"), axis=0, tiled=True),
    )
    qkv_mat, proj_mat, up_mat, down_mat, packed = unpack(gathered)
    gain_one, shift_one, qkv_bias, proj_bias, gain_two, shift_two, up_bias, down_bias = (
        split_vectors(packed)
    )
    inputs = tokens.astype(jnp.float32)
    tok_rows = inputs.shape[0]
    clips = tok_rows // CLIP_LEN
    normed = layer_norm(inputs, gain_one, shift_one).astype(jnp.bfloat16)
    qkv_all = (jnp.dot(normed, qkv_mat, preferred_element_type=jnp.float32) + qkv_bias).astype(
        jnp.bfloat16
    )
    qkv_clips = qkv_all.reshape(clips, CLIP_LEN, 3 * D)
    attended, lse_all = lax.map(attend_forward, qkv_clips)
    attended = attended.reshape(tok_rows, D).astype(jnp.bfloat16)
    hidden_res = (
        inputs + jnp.dot(attended, proj_mat, preferred_element_type=jnp.float32) + proj_bias
    )
    normed_two = layer_norm(hidden_res, gain_two, shift_two).astype(jnp.bfloat16)
    pre_act = jnp.dot(normed_two, up_mat, preferred_element_type=jnp.float32) + up_bias
    activ = jax.nn.gelu(pre_act).astype(jnp.bfloat16)
    output = (
        hidden_res + jnp.dot(activ, down_mat, preferred_element_type=jnp.float32) + down_bias
    ).astype(jnp.bfloat16)
    regathered = (
        lax.all_gather(qkv_weight.astype(jnp.bfloat16), ("dp", "fsdp"), axis=0, tiled=True),
        lax.all_gather(proj_weight.astype(jnp.bfloat16), ("dp", "fsdp"), axis=0, tiled=True),
        lax.all_gather(up_weight.astype(jnp.bfloat16), ("dp", "fsdp"), axis=0, tiled=True),
        lax.all_gather(down_weight.astype(jnp.bfloat16), ("dp", "fsdp"), axis=0, tiled=True),
        lax.all_gather(vectors.astype(jnp.bfloat16), ("dp", "fsdp"), axis=0, tiled=True),
    )
    qkv_mat, proj_mat, up_mat, down_mat, packed = unpack(regathered)
    gain_one, shift_one, qkv_bias, proj_bias, gain_two, shift_two, up_bias, down_bias = (
        split_vectors(packed)
    )
    frame_of = (jnp.arange(CLIP_LEN) // FRAME_TOK)[None, :]
    keep_rows = (frame_of >= cond_frames[:, None]).astype(jnp.float32).reshape(tok_rows, 1)
    back = cotangent.astype(jnp.float32) * keep_rows
    back_low = back.astype(jnp.bfloat16)
    grad_down = jnp.dot(activ.T, back_low, preferred_element_type=jnp.float32)
    grad_down_bias = jnp.sum(back, axis=0)
    grad_act = jnp.dot(back_low, down_mat.T, preferred_element_type=jnp.float32)
    _, gelu_pull = jax.vjp(jax.nn.gelu, pre_act)
    grad_pre = gelu_pull(grad_act)[0].astype(jnp.bfloat16)
    grad_up = jnp.dot(normed_two.T, grad_pre, preferred_element_type=jnp.float32)
    grad_up_bias = jnp.sum(grad_pre.astype(jnp.float32), axis=0)
    grad_normed_two = jnp.dot(grad_pre, up_mat.T, preferred_element_type=jnp.float32)
    _, second_pull = jax.vjp(layer_norm, hidden_res, gain_two, shift_two)
    grad_res, grad_gain_two, grad_shift_two = second_pull(grad_normed_two)
    grad_res = grad_res + back
    grad_branch = grad_res.astype(jnp.bfloat16)
    grad_proj = jnp.dot(attended.T, grad_branch, preferred_element_type=jnp.float32)
    grad_proj_bias = jnp.sum(grad_branch.astype(jnp.float32), axis=0)
    grad_att = jnp.dot(grad_branch, proj_mat.T, preferred_element_type=jnp.float32).astype(
        jnp.bfloat16
    )
    grad_qkv = lax.map(attend_backward, (qkv_clips, grad_att.reshape(clips, CLIP_LEN, D), lse_all))
    grad_qkv = grad_qkv.reshape(tok_rows, 3 * D)
    grad_qkv_mat = jnp.dot(normed.T, grad_qkv, preferred_element_type=jnp.float32)
    grad_qkv_bias = jnp.sum(grad_qkv.astype(jnp.float32), axis=0)
    grad_normed = jnp.dot(grad_qkv, qkv_mat.T, preferred_element_type=jnp.float32)
    _, first_pull = jax.vjp(layer_norm, inputs, gain_one, shift_one)
    grad_in, grad_gain_one, grad_shift_one = first_pull(grad_normed)
    input_grad = grad_res + grad_in
    grad_packed = jnp.concatenate(
        [
            grad_gain_one,
            grad_shift_one,
            grad_qkv_bias,
            grad_proj_bias,
            grad_gain_two,
            grad_shift_two,
            grad_up_bias,
            grad_down_bias,
        ]
    ).reshape(shards, -1)
    summed_qkv, summed_proj, summed_up, summed_down, summed_vec = (
        lax.psum_scatter(
            grad_qkv_mat.reshape(shards, -1), ("dp", "fsdp"), scatter_dimension=0, tiled=True
        ),
        lax.psum_scatter(
            grad_proj.reshape(shards, -1), ("dp", "fsdp"), scatter_dimension=0, tiled=True
        ),
        lax.psum_scatter(
            grad_up.reshape(shards, -1), ("dp", "fsdp"), scatter_dimension=0, tiled=True
        ),
        lax.psum_scatter(
            grad_down.reshape(shards, -1), ("dp", "fsdp"), scatter_dimension=0, tiled=True
        ),
        lax.psum_scatter(grad_packed, ("dp", "fsdp"), scatter_dimension=0, tiled=True),
    )
    qkv_f, qkv_s, qkv_w, qkv_e = adamw(
        qkv_weight, summed_qkv, qkv_first, qkv_second, qkv_average, RATE_MATRIX, WEIGHT_DECAY
    )
    proj_f, proj_s, proj_w, proj_e = adamw(
        proj_weight, summed_proj, proj_first, proj_second, proj_average, RATE_MATRIX, WEIGHT_DECAY
    )
    up_f, up_s, up_w, up_e = adamw(
        up_weight, summed_up, up_first, up_second, up_average, RATE_MATRIX, WEIGHT_DECAY
    )
    down_f, down_s, down_w, down_e = adamw(
        down_weight, summed_down, down_first, down_second, down_average, RATE_MATRIX, WEIGHT_DECAY
    )
    vec_f, vec_s, vec_w, vec_e = adamw(
        vectors, summed_vec, vector_first, vector_second, vector_average, RATE_VECTOR, 0.0
    )
    return (
        output,
        input_grad,
        qkv_f,
        qkv_s,
        qkv_w,
        qkv_e,
        proj_f,
        proj_s,
        proj_w,
        proj_e,
        up_f,
        up_s,
        up_w,
        up_e,
        down_f,
        down_s,
        down_w,
        down_e,
        vec_f,
        vec_s,
        vec_w,
        vec_e,
    )


def solution(mesh):
    return jax.shard_map(
        local,
        mesh=mesh,
        in_specs=(
            P(("dp", "fsdp"), None),
            P(("dp", "fsdp"), None),
            P(("dp", "fsdp")),
            P(("dp", "fsdp"), None),
            P(("dp", "fsdp"), None),
            P(("dp", "fsdp"), None),
            P(("dp", "fsdp"), None),
            P(("dp", "fsdp"), None),
            P(("dp", "fsdp"), None),
            P(("dp", "fsdp"), None),
            P(("dp", "fsdp"), None),
            P(("dp", "fsdp"), None),
            P(("dp", "fsdp"), None),
            P(("dp", "fsdp"), None),
            P(("dp", "fsdp"), None),
            P(("dp", "fsdp"), None),
            P(("dp", "fsdp"), None),
            P(("dp", "fsdp"), None),
            P(("dp", "fsdp"), None),
            P(("dp", "fsdp"), None),
            P(("dp", "fsdp"), None),
            P(("dp", "fsdp"), None),
            P(("dp", "fsdp"), None),
        ),
        out_specs=(
            P(("dp", "fsdp"), None),
            P(("dp", "fsdp"), None),
            P(("dp", "fsdp"), None),
            P(("dp", "fsdp"), None),
            P(("dp", "fsdp"), None),
            P(("dp", "fsdp"), None),
            P(("dp", "fsdp"), None),
            P(("dp", "fsdp"), None),
            P(("dp", "fsdp"), None),
            P(("dp", "fsdp"), None),
            P(("dp", "fsdp"), None),
            P(("dp", "fsdp"), None),
            P(("dp", "fsdp"), None),
            P(("dp", "fsdp"), None),
            P(("dp", "fsdp"), None),
            P(("dp", "fsdp"), None),
            P(("dp", "fsdp"), None),
            P(("dp", "fsdp"), None),
            P(("dp", "fsdp"), None),
            P(("dp", "fsdp"), None),
            P(("dp", "fsdp"), None),
            P(("dp", "fsdp"), None),
        ),
        check_vma=False,
    )
```

profile of v0, /device:TPU:0, one launch (start us, length us, event | category | flops | bytes accessed | tf_op | source)
XLA Modules:
  0.0 691.6 jit_solution(16010319877557200792)
XLA Ops:
  13.1 43.2 %all-gather = bf16[32,1,208]{2,1,0:T(2,128)(2,1)S(1)} all-gather(bf16[1,1,208]{2,1,0:T(2,128)(2,1)S(1)} %convert_bitcast_fusion.4), channel_id=1, replica_groups=mesh['dp'=8,'fsdp'=4] {'dp','fsdp'}, dimensions={0}, use_global_device_ids=true | all-gather | bytes 13728 | tf_op jit(solution)/shard_map/all_gather | solution.py:177
  59.9 41.0 %all-gather.2 = bf16[32,1,8192]{2,1,0:T(2,128)(2,1)S(1)} all-gather(bf16[1,1,8192]{2,1,0:T(2,128)(2,1)S(1)} %convert_bitcast_fusion.3), channel_id=1, replica_groups=mesh['dp'=8,'fsdp'=4] {'dp','fsdp'}, dimensions={0}, use_global_device_ids=true | all-gather | bytes 540672 | tf_op jit(solution)/shard_map/all_gather | solution.py:174
  100.9 3.2 reduce.13
  105.1 3.1 copy.83
  109.8 4.0 copy.87
  113.8 12.3 %reduce.12 = bf16[32,24576]{1,0:T(8,128)(2,1)} reduce(bf16[32,1,24576]{2,1,0:T(2,128)(2,1)} %all-gather.9.cloned.1.call-done, bf16[]{:T(256)} %constant.348), dimensions={1}, to_apply=%all-gather.1.reduce_sub_computation | reduce | bytes 3145730 | tf_op jit(solution)/shard_map/all_gather | solution.py:173
  126.1 2.7 reshape.466
  128.9 7.5 %add_convert_fusion = bf16[2048,1536]{1,0:T(8,128)(2,1)} fusion(bf16[512,1536]{1,0:T(8,128)(2,1)} %reshape.466, f32[1536]{0:T(1024)S(1)} %slice-done.2, bf16[2048,512]{0,1:T(8,128)(2,1)S(1)} %copy.83, f32[512]{0:T(512)S(1)} %get-tuple-element.381, f32[512]{0:T(512)S(1)} %get-tuple-element.382, f32[2048]{0:T(1024)S(1)} %fusion.64, ...), kind=kOutput, calls=%fused_computation.75 | convolution fusion | flops 3233808384 | bytes 9988096 | tf_op jit(solution)/shard_map/dot_general | solution.py:187
  136.4 8.7 %copy.84 = bf16[2,1024,1536]{1,2,0:T(8,128)(2,1)} copy(bf16[2,1024,1536]{2,1,0:T(8,128)(2,1)} %bitcast.246) | data formatting | bytes 12582912 | tf_op jit(solution)/shard_map/while | solution.py:191
  145.1 47.4 %while.31 = (s32[]{:T(128)}, bf16[2,1024,512]{2,1,0:T(8,128)(2,1)}, f32[2,8,1024]{2,1,0:T(8,128)S(1)}, bf16[2,1024,1536]{1,2,0:T(8,128)(2,1)}, s32[]{:T(128)}) while((s32[]{:T(128)}, bf16[2,1024,512]{2,1,0:T(8,128)(2,1)}, f32[2,8,1024]{2,1,0:T(8,128)S(1)}, bf16[2,1024,1536]{1,2,0:T(8,128)(2,1)}, s32[]{:T(128)}) %tuple.152), condition=%wide.region_7.8_spmd, body=%wide.region_2.7_spmd.sunk | while | flops 1688994304 | bytes 105189456 | solution.py:191
  153.9 3.1 fusion.188
  157.0 4.4 fusion.189
  161.4 5.6 fusion.190
  175.0 2.5 fusion.193
  177.5 3.1 fusion.188
  180.6 4.4 fusion.189
  185.0 5.6 fusion.190
  192.5 3.8 fusion.88
  198.9 12.5 %reduce.14 = bf16[32,32768]{1,0:T(8,128)(2,1)S(1)} reduce(bf16[32,1,32768]{2,1,0:T(2,128)(2,1)} %all-gather.11.cloned.1.call-done, bf16[]{:T(256)} %constant.348), dimensions={1}, to_apply=%all-gather.3.reduce_sub_computation | reduce | bytes 4194306 | tf_op jit(solution)/shard_map/all_gather | solution.py:175
  213.9 12.5 %reduce.10 = bf16[32,32768]{1,0:T(8,128)(2,1)S(1)} reduce(bf16[32,1,32768]{2,1,0:T(2,128)(2,1)} %all-gather.13.cloned.1.call-done, bf16[]{:T(256)} %constant.348), dimensions={1}, to_apply=%all-gather.4.reduce_sub_computation | reduce | bytes 4194306 | tf_op jit(solution)/shard_map/all_gather | solution.py:176
  228.8 16.3 %multiply_convert_fusion.2 = (bf16[2048,2048]{1,0:T(8,128)(2,1)}, f32[2048,2048]{1,0:T(8,128)}) fusion(f32[2048]{0:T(1024)S(1)} %copy-done.60, bf16[512,2048]{1,0:T(8,128)(2,1)} %reshape.469, f32[2048,512]{0,1:T(8,128)} %copy-done.8, f32[512]{0:T(512)S(1)} %copy-done.65, f32[512]{0:T(512)S(1)} %copy-done.56, f32[2048]{0:T(1024)S(1)} %fusion.65, ...), kind=kOutput, calls=%fused_computation.73 | convolution fusion | flops 4342153216 | bytes 31485952 | tf_op jit(solution)/shard_map/dot_general | solution.py:197
  245.1 19.9 %convert_reduce_fusion = (f32[2048]{0:T(1024)}, bf16[2048,2048]{1,0:T(8,128)(2,1)}) fusion(f32[2048,2048]{1,0:T(8,128)} %get-tuple-element.386, f32[2048]{0:T(1024)S(1)} %copy-done.60, bf16[2048,512]{1,0:T(8,128)(2,1)S(1)} %copy-done.19, bf16[2048,512]{0,1:T(8,128)(2,1)S(1)} %copy-done.16, f32[2048]{0:T(1024)S(1)} %bitcast.247), kind=kOutput, calls=%fused_computation.72 | convolution fusion | flops 4394579968 | bytes 29384704 | tf_op jit(solution)/shard_map/dot_general | solution.py:219
  264.9 10.3 %fusion.90 = (f32[512]{0:T(512)}, f32[2048,512]{1,0:T(8,128)}) fusion(bf16[2048,2048]{1,0:T(8,128)(2,1)} %get-tuple-element.392, bf16[512,2048]{1,0:T(8,128)(2,1)S(1)} %copy-done.20), kind=kOutput, calls=%fused_computation.180 | convolution fusion | flops 4296015360 | bytes 14682112 | tf_op jit(solution)/shard_map/dot_general | solution.py:224
  275.2 6.3 fusion.73
  281.5 5.8 copy.88
  287.4 5.4 multiply_reduce_fusion.2
  299.3 2.7 convolution_convert_fusion
  302.0 6.8 fusion.55
  308.8 5.0 reshape.476
  313.7 5.0 reshape.475
  319.9 106.6 %while.32 = (s32[]{:T(128)}, bf16[2,1024,1536]{1,2,0:T(8,128)(2,1)}, bf16[2,1024,1536]{1,2,0:T(8,128)(2,1)}, f32[2,8,1024]{2,1,0:T(8,128)S(1)}, bf16[2,1024,512]...) while((s32[]{:T(128)}, bf16[2,1024,1536]{1,2,0:T(8,128)(2,1)}, bf16[2,1024,1536]{1,2,0:T(8,128)(2,1)}, ...), condition=%wide.region_15.16_spmd, body=%wide.region_12.15_spmd.sunk | while | flops 4111983104 | bytes 304419296 | solution.py:234
  328.9 3.3 fusion.218
  332.1 2.9 multiply_reduce_fusion.7
  335.1 2.7 multiply_convert_fusion.5
  341.8 4.6 subtract_exponential_fusion.5
  346.4 2.6 fusion.220
  349.0 9.0 %multiply_reduce_fusion.8 = (f32[8,512]{1,0:T(8,128)}, f32[8,512,1024]{2,1,0:T(8,128)}) fusion(f32[8,512,1024]{2,1,0:T(8,128)S(1)} %subtract_exponential_fusion.5, bf16[512,8,64]{0,2,1:T(8,128)(2,1)S(1)} %bitcast.219, bf16[1024,8,64]{0,2,1:T(8,128)(2,1)} %bitcast.228), kind=kOutput, calls=%fused_computation.29.clone.1 | convolution fusion | flops 545255424 | bytes 35143680 | tf_op jit(solution)/shard_map/while/body/eval_jaxpr/qhd,khd->hqk/dot_general | solution.py:115
  358.0 7.1 %multiply_convert_fusion.6 = bf16[8,512,1024]{2,1,0:T(8,128)(2,1)S(1)} fusion(f32[8,512,1024]{2,1,0:T(8,128)S(1)} %subtract_exponential_fusion.5, f32[8,512,1024]{2,1,0:T(8,128)} %get-tuple-element.503, f32[8,512]{1,0:T(8,128)} %get-tuple-element.504), kind=kLoop, calls=%fused_computation.28.clone.1 | loop fusion | flops 12582912 | bytes 41959424 | tf_op jit(solution)/shard_map/while/body/eval_jaxpr/convert_element_type | solution.py:119
  365.1 2.7 fusion.223
  370.5 2.6 copy-done.15
  381.9 3.3 fusion.218
  385.2 2.9 multiply_reduce_fusion.7
  388.1 2.7 multiply_convert_fusion.5
  394.8 4.6 subtract_exponential_fusion.5
  399.4 2.6 fusion.220
  402.0 9.0 %multiply_reduce_fusion.8 = (f32[8,512]{1,0:T(8,128)}, f32[8,512,1024]{2,1,0:T(8,128)}) fusion(f32[8,512,1024]{2,1,0:T(8,128)S(1)} %subtract_exponential_fusion.5, bf16[512,8,64]{0,2,1:T(8,128)(2,1)S(1)} %bitcast.219, bf16[1024,8,64]{0,2,1:T(8,128)(2,1)} %bitcast.228), kind=kOutput, calls=%fused_computation.29.clone.1 | convolution fusion | flops 545255424 | bytes 35143680 | tf_op jit(solution)/shard_map/while/body/eval_jaxpr/qhd,khd->hqk/dot_general | solution.py:115
  411.0 7.1 %multiply_convert_fusion.6 = bf16[8,512,1024]{2,1,0:T(8,128)(2,1)S(1)} fusion(f32[8,512,1024]{2,1,0:T(8,128)S(1)} %subtract_exponential_fusion.5, f32[8,512,1024]{2,1,0:T(8,128)} %get-tuple-element.503, f32[8,512]{1,0:T(8,128)} %get-tuple-element.504), kind=kLoop, calls=%fused_computation.28.clone.1 | loop fusion | flops 12582912 | bytes 41959424 | tf_op jit(solution)/shard_map/while/body/eval_jaxpr/convert_element_type | solution.py:119
  418.1 2.7 fusion.223
  423.5 2.6 copy-done.15
  426.6 8.8 %copy.91 = bf16[2,1024,1536]{2,1,0:T(8,128)(2,1)} copy(bf16[2,1024,1536]{1,2,0:T(8,128)(2,1)} %get-tuple-element.205) | data formatting | bytes 12582912 | tf_op jit(solution)/shard_map/while | solution.py:234
  435.4 7.9 %fusion.70 = f32[512,1536]{1,0:T(8,128)} fusion(bf16[2048,1536]{1,0:T(8,128)(2,1)} %bitcast.244, bf16[2048,512]{0,1:T(8,128)(2,1)S(1)} %copy-done.5, f32[512]{0:T(512)S(1)} %copy-done.64, f32[512]{0:T(512)S(1)} %copy-done.54, f32[2048]{0:T(1024)S(1)} %copy-done.45, f32[2048]{0:T(1024)S(1)} %copy-done.30), kind=kOutput, calls=%fused_computation.168 | convolution fusion | flops 3227516928 | bytes 11554816 | tf_op jit(solution)/shard_map/dot_general | solution.py:236
  443.3 3.3 reshape.473
  447.3 12.1 %add_convert_fusion.1 = bf16[2048,512]{0,1:T(8,128)(2,1)} fusion(f32[2048,512]{0,1:T(8,128)} %copy-done.8, bf16[2048,2048]{1,0:T(8,128)(2,1)} %get-tuple-element.385, bf16[2048,512]{1,0:T(8,128)(2,1)} %reshape.470, f32[512]{0:T(512)S(1)} %copy-done.62), kind=kOutput, calls=%fused_computation.101 | convolution fusion | flops 4298113024 | bytes 16779264 | tf_op jit(solution)/shard_map/dot_general | solution.py:200
  459.3 4.0 copy.95
  463.3 8.9 %fusion.89 = (f32[512]{0:T(512)S(1)}, f32[2048,512]{1,0:T(8,128)}) fusion(bf16[2048,1536]{1,0:T(8,128)(2,1)} %bitcast.245, bf16[512,1536]{1,0:T(8,128)(2,1)} %reshape.466), kind=kOutput, calls=%fused_computation.179 | convolution fusion | flops 3222273536 | bytes 12060672 | tf_op jit(solution)/shard_map/dot_general | solution.py:238
  472.2 5.5 copy.92
  477.8 3.2 fusion.50
  483.5 4.1 convert_reduce_fusion.1
  488.7 3.7 fusion.52
  492.7 5.7 copy.96
  498.4 37.3 %all-reduce.6 = f32[32,208]{1,0:T(8,128)S(1)} all-reduce(f32[32,208]{1,0:T(8,128)S(1)} %reshape.477), channel_id=6, replica_groups=mesh['dp'=8,'fsdp'=4] {'dp','fsdp'}, use_global_device_ids=true, to_apply=%region_30.31.clone | all-reduce | flops 6656 | bytes 53248
  536.3 139.6 %all-reduce.10.cloned.1.call-done = (f32[32,24576]{1,0:T(8,128)}, f32[32,8192]{1,0:T(8,128)}, f32[32,32768]{1,0:T(8,128)}, f32[32,32768]{1,0:T(8,128)}) async-done(((f32[32,24576]{1,0:T(8,128)}, f32[32,8192]{1,0:T(8,128)}, f32[32,32768]{1,0:T(8,128)}, f32[32,32768]{1,0:T(8,128)}), (f32[32,24576]{1,0:T(8,128)}, f32[32,8192]{1,0:T(8,128)}, f32[32,32768]{1,0:T(8,128)}, ...) | async-done | bytes 12582928
  675.8 2.6 multiply_add_fusion.4
  680.4 4.4 multiply_add_fusion
  (301 shorter events, 82.9 us)
Async XLA Ops:
  7.2 106.6 %all-gather.9.cloned.1.call-start = ((), (), s32[]{:S(2)}) async-start(), calls=%async_computation | async-start | bytes 3244032 | tf_op jit(solution)/shard_map/all_gather | solution.py:173
  8.9 190.0 %all-gather.11.cloned.1.call-start = ((), (), s32[]{:S(2)}) async-start(), calls=%async_computation.1 | async-start | bytes 4325376 | tf_op jit(solution)/shard_map/all_gather | solution.py:175
  10.6 203.3 %all-gather.13.cloned.1.call-start = ((), (), s32[]{:S(2)}) async-start(), calls=%async_computation.2 | async-start | bytes 4325376 | tf_op jit(solution)/shard_map/all_gather | solution.py:176
  12.3 663.5 %all-reduce.10.cloned.1.call-start = ((), (), s32[]{:S(2)}) async-start(), calls=%async_computation.3 | async-start | bytes 25165824
  56.5 52.1 %copy-start.38 = (f32[6656]{0:T(1024)}, f32[6656]{0:T(1024)S(1)}, u32[]{:S(2)}) copy-start(f32[6656]{0:T(1024)S(1)} %reshape.478) | copy-start | bytes 79876
  57.7 71.1 %copy-start.53 = (f32[512]{0:T(512)}, f32[512]{0:T(512)S(1)}, u32[]{:S(2)}) copy-start(f32[512]{0:T(512)S(1)} %get-tuple-element.382) | copy-start | bytes 6148
  57.7 71.2 %copy-start.63 = (f32[512]{0:T(512)}, f32[512]{0:T(512)S(1)}, u32[]{:S(2)}) copy-start(f32[512]{0:T(512)S(1)} %get-tuple-element.381) | copy-start | bytes 6148
  108.2 28.2 %copy-start.4 = (bf16[2048,512]{0,1:T(8,128)(2,1)}, bf16[2048,512]{0,1:T(8,128)(2,1)S(1)}, u32[]{:S(2)}) copy-start(bf16[2048,512]{0,1:T(8,128)(2,1)S(1)} %copy.83) | copy-start | bytes 6291460
  108.6 20.3 %copy-start.29 = (f32[2048]{0:T(1024)}, f32[2048]{0:T(1024)S(1)}, u32[]{:S(2)}) copy-start(f32[2048]{0:T(1024)S(1)} %broadcast_multiply_fusion.1) | copy-start | bytes 24580
  109.8 19.1 %copy-start.44 = (f32[2048]{0:T(1024)}, f32[2048]{0:T(1024)S(1)}, u32[]{:S(2)}) copy-start(f32[2048]{0:T(1024)S(1)} %fusion.64) | copy-start | bytes 24580
  113.8 15.1 %slice-start.2 = ((f32[6656]{0:T(1024)}), f32[1536]{0:T(1024)S(1)}, s32[]{:S(2)}) async-start(f32[6656]{0:T(1024)} %copy-done.38), calls=%async_computation.6 | async-start | bytes 16384 | tf_op jit(solution)/shard_map/slice | solution.py:35
  145.1 47.4 %copy-start.23 = (bf16[512,512]{1,0:T(8,128)(2,1)S(1)}, bf16[512,512]{1,0:T(8,128)(2,1)}, u32[]{:S(2)}) copy-start(bf16[512,512]{1,0:T(8,128)(2,1)} %reshape.468) | copy-start | bytes 1572868
  145.1 47.4 %copy-start.66 = (f32[512]{0:T(512)S(1)}, f32[512]{0:T(512)}, u32[]{:S(2)}) copy-start(f32[512]{0:T(512)} %get-tuple-element.380) | copy-start | bytes 6148
  213.8 14.9 %copy-start.56 = (f32[512]{0:T(512)S(1)}, f32[512]{0:T(512)}, u32[]{:S(2)}) copy-start(f32[512]{0:T(512)} %get-tuple-element.379) | copy-start | bytes 6148
  213.8 14.9 %copy-start.60 = (f32[2048]{0:T(1024)S(1)}, f32[2048]{0:T(1024)}, u32[]{:S(2)}) copy-start(f32[2048]{0:T(1024)} %slice.265) | copy-start | bytes 24580
  213.8 14.9 %copy-start.65 = (f32[512]{0:T(512)S(1)}, f32[512]{0:T(512)}, u32[]{:S(2)}) copy-start(f32[512]{0:T(512)} %get-tuple-element.378) | copy-start | bytes 6148
  228.7 16.3 %copy-start.16 = (bf16[2048,512]{0,1:T(8,128)(2,1)S(1)}, bf16[2048,512]{0,1:T(8,128)(2,1)}, u32[]{:S(2)}) copy-start(bf16[2048,512]{0,1:T(8,128)(2,1)} %copy.87) | copy-start | bytes 6291460
  228.7 16.3 %copy-start.19 = (bf16[2048,512]{1,0:T(8,128)(2,1)S(1)}, bf16[2048,512]{1,0:T(8,128)(2,1)}, u32[]{:S(2)}) copy-start(bf16[2048,512]{1,0:T(8,128)(2,1)} %reshape.470) | copy-start | bytes 6291460
  228.8 16.3 %copy-start.42 = (f32[1,8,2,128]{3,1,2,0:T(8,128)S(1)}, f32[1,8,2,128]{3,1,2,0:T(8,128)}, u32[]{:S(2)}) copy-start(f32[1,8,2,128]{3,1,2,0:T(8,128)} %copy.125) | copy-start | bytes 24580
  245.0 19.9 %copy-start.20 = (bf16[512,2048]{1,0:T(8,128)(2,1)S(1)}, bf16[512,2048]{1,0:T(8,128)(2,1)}, u32[]{:S(2)}) copy-start(bf16[512,2048]{1,0:T(8,128)(2,1)} %reshape.469) | copy-start | bytes 6291460
  264.9 10.3 %copy-start.9 = (f32[2048,512]{0,1:T(8,128)S(1)}, f32[2048,512]{0,1:T(8,128)}, u32[]{:S(2)}) copy-start(f32[2048,512]{0,1:T(8,128)} %copy-done.8) | copy-start | bytes 12582916
  264.9 10.3 %copy-start.72 = (bf16[2048,2048]{1,0:T(8,128)(2,1)S(1)}, bf16[2048,2048]{1,0:T(8,128)(2,1)}, u32[]{:S(2)}) copy-start(bf16[2048,2048]{1,0:T(8,128)(2,1)} %get-tuple-element.392) | copy-start | bytes 25165828
  287.4 5.4 copy-start.10
  287.4 5.9 copy-start.11
  337.7 4.0 copy-start.1
  341.8 4.6 copy-start.14
  358.0 7.1 %copy-start.2 = (bf16[1024,512]{0,1:T(8,128)(2,1)S(1)}, bf16[1024,512]{0,1:T(8,128)(2,1)}, u32[]{:S(2)}) copy-start(bf16[1024,512]{0,1:T(8,128)(2,1)} %get-tuple-element.497) | copy-start | bytes 3145732 | tf_op jit(solution)/shard_map/while
  365.1 4.5 slice-start
  394.8 4.6 copy-start.14
  411.0 7.1 %copy-start.2 = (bf16[1024,512]{0,1:T(8,128)(2,1)S(1)}, bf16[1024,512]{0,1:T(8,128)(2,1)}, u32[]{:S(2)}) copy-start(bf16[1024,512]{0,1:T(8,128)(2,1)} %get-tuple-element.497) | copy-start | bytes 3145732 | tf_op jit(solution)/shard_map/while
  418.1 4.5 slice-start
  426.5 8.8 %copy-start.5 = (bf16[2048,512]{0,1:T(8,128)(2,1)S(1)}, bf16[2048,512]{0,1:T(8,128)(2,1)}, u32[]{:S(2)}) copy-start(bf16[2048,512]{0,1:T(8,128)(2,1)} %copy-done.4) | copy-start | bytes 6291460
  426.5 8.8 %copy-start.30 = (f32[2048]{0:T(1024)S(1)}, f32[2048]{0:T(1024)}, u32[]{:S(2)}) copy-start(f32[2048]{0:T(1024)} %copy-done.29) | copy-start | bytes 24580
  426.5 8.8 %copy-start.45 = (f32[2048]{0:T(1024)S(1)}, f32[2048]{0:T(1024)}, u32[]{:S(2)}) copy-start(f32[2048]{0:T(1024)} %copy-done.44) | copy-start | bytes 24580
  426.5 8.8 %copy-start.54 = (f32[512]{0:T(512)S(1)}, f32[512]{0:T(512)}, u32[]{:S(2)}) copy-start(f32[512]{0:T(512)} %copy-done.53) | copy-start | bytes 6148
  426.5 8.8 %copy-start.64 = (f32[512]{0:T(512)S(1)}, f32[512]{0:T(512)}, u32[]{:S(2)}) copy-start(f32[512]{0:T(512)} %copy-done.63) | copy-start | bytes 6148
  483.4 4.2 copy-start.58
  483.4 4.2 copy-start.57
  483.4 4.2 copy-start.67
  483.5 4.2 copy-start.59
  483.5 4.5 copy-start.13
  483.5 5.2 copy-start.17
  483.5 5.2 copy-start.43
  483.5 5.2 copy-start.47
  492.4 43.2 %copy-start.61 = (f32[1,208]{1,0:T(1,128)S(1)}, f32[1,208]{1,0:T(1,128)}, u32[]{:S(2)}) copy-start(f32[1,208]{1,0:T(1,128)} %param.46) | copy-start | bytes 2500
  492.5 43.2 %copy-start.68 = (f32[1,208]{1,0:T(1,128)S(1)}, f32[1,208]{1,0:T(1,128)}, u32[]{:S(2)}) copy-start(f32[1,208]{1,0:T(1,128)} %param.61) | copy-start | bytes 2500
  492.5 43.2 %copy-start.69 = (f32[1,208]{1,0:T(1,128)S(1)}, f32[1,208]{1,0:T(1,128)}, u32[]{:S(2)}) copy-start(f32[1,208]{1,0:T(1,128)} %param.56) | copy-start | bytes 2500
  492.5 43.2 %copy-start.70 = (f32[1,208]{1,0:T(1,128)S(1)}, f32[1,208]{1,0:T(1,128)}, u32[]{:S(2)}) copy-start(f32[1,208]{1,0:T(1,128)} %param.51) | copy-start | bytes 2500
  492.5 183.3 %copy-start.28 = (f32[1,24576]{1,0:T(1,128)S(1)}, f32[1,24576]{1,0:T(1,128)}, u32[]{:S(2)}) copy-start(f32[1,24576]{1,0:T(1,128)} %param.42) | copy-start | bytes 294916
  492.5 183.3 %copy-start.39 = (f32[1,24576]{1,0:T(1,128)S(1)}, f32[1,24576]{1,0:T(1,128)}, u32[]{:S(2)}) copy-start(f32[1,24576]{1,0:T(1,128)} %param.57) | copy-start | bytes 294916
  492.5 183.3 %copy-start.40 = (f32[1,24576]{1,0:T(1,128)S(1)}, f32[1,24576]{1,0:T(1,128)}, u32[]{:S(2)}) copy-start(f32[1,24576]{1,0:T(1,128)} %param.52) | copy-start | bytes 294916
  492.5 183.3 %copy-start.41 = (f32[1,24576]{1,0:T(1,128)S(1)}, f32[1,24576]{1,0:T(1,128)}, u32[]{:S(2)}) copy-start(f32[1,24576]{1,0:T(1,128)} %param.47) | copy-start | bytes 294916
  492.5 185.9 %copy-start.37 = (f32[1,8192]{1,0:T(1,128)S(1)}, f32[1,8192]{1,0:T(1,128)}, u32[]{:S(2)}) copy-start(f32[1,8192]{1,0:T(1,128)} %param.43) | copy-start | bytes 98308
  492.6 185.9 %copy-start.50 = (f32[1,8192]{1,0:T(1,128)S(1)}, f32[1,8192]{1,0:T(1,128)}, u32[]{:S(2)}) copy-start(f32[1,8192]{1,0:T(1,128)} %param.58) | copy-start | bytes 98308
  492.6 185.9 %copy-start.51 = (f32[1,8192]{1,0:T(1,128)S(1)}, f32[1,8192]{1,0:T(1,128)}, u32[]{:S(2)}) copy-start(f32[1,8192]{1,0:T(1,128)} %param.53) | copy-start | bytes 98308
  492.6 185.9 %copy-start.52 = (f32[1,8192]{1,0:T(1,128)S(1)}, f32[1,8192]{1,0:T(1,128)}, u32[]{:S(2)}) copy-start(f32[1,8192]{1,0:T(1,128)} %param.48) | copy-start | bytes 98308
  492.6 187.8 %copy-start.21 = (f32[1,32768]{1,0:T(1,128)S(1)}, f32[1,32768]{1,0:T(1,128)}, u32[]{:S(2)}) copy-start(f32[1,32768]{1,0:T(1,128)} %param.44) | copy-start | bytes 393220
  492.6 187.8 %copy-start.22 = (f32[1,32768]{1,0:T(1,128)S(1)}, f32[1,32768]{1,0:T(1,128)}, u32[]{:S(2)}) copy-start(f32[1,32768]{1,0:T(1,128)} %param.45) | copy-start | bytes 393220
  492.6 187.8 %copy-start.31 = (f32[1,32768]{1,0:T(1,128)S(1)}, f32[1,32768]{1,0:T(1,128)}, u32[]{:S(2)}) copy-start(f32[1,32768]{1,0:T(1,128)} %param.60) | copy-start | bytes 393220
  492.6 187.7 %copy-start.32 = (f32[1,32768]{1,0:T(1,128)S(1)}, f32[1,32768]{1,0:T(1,128)}, u32[]{:S(2)}) copy-start(f32[1,32768]{1,0:T(1,128)} %param.55) | copy-start | bytes 393220
  492.6 187.7 %copy-start.33 = (f32[1,32768]{1,0:T(1,128)S(1)}, f32[1,32768]{1,0:T(1,128)}, u32[]{:S(2)}) copy-start(f32[1,32768]{1,0:T(1,128)} %param.50) | copy-start | bytes 393220
  492.6 187.7 %copy-start.34 = (f32[1,32768]{1,0:T(1,128)S(1)}, f32[1,32768]{1,0:T(1,128)}, u32[]{:S(2)}) copy-start(f32[1,32768]{1,0:T(1,128)} %param.54) | copy-start | bytes 393220
  492.7 187.7 %copy-start.35 = (f32[1,32768]{1,0:T(1,128)S(1)}, f32[1,32768]{1,0:T(1,128)}, u32[]{:S(2)}) copy-start(f32[1,32768]{1,0:T(1,128)} %param.49) | copy-start | bytes 393220
  492.7 187.7 %copy-start.36 = (f32[1,32768]{1,0:T(1,128)S(1)}, f32[1,32768]{1,0:T(1,128)}, u32[]{:S(2)}) copy-start(f32[1,32768]{1,0:T(1,128)} %param.59) | copy-start | bytes 393220
  (31 other events, 85.2 us)
Sparse Core Ops, SparseCore 0:
  11.5 62.5 all-gather.8
  77.5 61.6 all-gather.10
  142.6 60.7 all-gather.12
  446.7 229.0 all-reduce.9
where the time goes:
time: 697 us; the launch traced here: 692 us
  matrix products  193 us (28%)
  waiting for transfers between devices  140 us (20%)
  blocking collectives  122 us (18%)
  other arithmetic  117 us (17%)
  local copies, waits for them, and re-layouts  104 us (15%)
  between operations  14.9 us (2%)
    unnamed x5, waiting for transfers between devices  140 us
    all_gather x1, blocking collectives, local(): lax.all_gather(vectors.astype(jnp.bfloat16), ('dp', 'fsdp'), axis=0, tile...  43.2 us
    all_gather x1, blocking collectives, local(): lax.all_gather(proj_weight.astype(jnp.bfloat16), ('dp', 'fsdp'), axis=0,...  41 us
    unnamed x1, blocking collectives  37.3 us
    unnamed x140, local copies, waits for them, and re-layouts  24.3 us
    dot_general x4, matrix products, attend_backward(): jnp.einsum('qhd,khd->hqk', go_block, values_part[:stop], preferred_elemen...  23.9 us
    dot_general x8, matrix products, block_scores(): jnp.einsum('qhd,khd->hqk', q_block, k_block, preferred_element_type=jnp.f...  20.9 us
    dot_general x1, matrix products, local(): grad_act = jnp.dot(back_low, down_mat.T, preferred_element_type=jnp.float32)  19.9 us
  transfers between devices with their start and end apart: 4, of which 1 were waited for; matrix products, arithmetic and copies ran while one was open for 24% of the time, Pallas kernels for 0%

commit v1 on v0

v1 whole, which is shorter than its diff:
```python
import functools
from types import SimpleNamespace

import jax
import jax.numpy as jnp
from jax import lax
from jax.experimental import pallas as pl
from jax.experimental.pallas import tpu as pltpu
from jax.sharding import PartitionSpec as P

D = 512
FF = 2048
HEADS = 8
HEAD_DIM = 64
FRAME_TOK = 64
STEP = 10
CLIP_LEN = 1024
VEC = 9 * D + FF

EPS = 1e-05
BETA_ONE = 0.9
BETA_TWO = 0.95
ADAM_EPS = 1e-08
RATE_MATRIX = 0.02
RATE_VECTOR = 0.2
WEIGHT_DECAY = 0.1
EMA_KEEP = 0.9
NEG = -1e30

AXES = ("dp", "fsdp")
MESH = pl.DeviceIdType.MESH
BF16 = jnp.bfloat16
F32 = jnp.float32
NN = (((1,), (0,)), ((), ()))
NT = (((1,), (1,)), ((), ()))
TN = (((0,), (0,)), ((), ()))
PAIRS = HEADS // 2
QB = 256
TILE = 512
CHUNK = 512
VROWS = 56
G1, S1, BQKV, BO, G2, S2, B1, B2 = 0, 4, 8, 20, 24, 28, 32, 48
GELU_A = 0.7978845608028654
GELU_B = 0.044715


def dot(left, right, dims=NN):
    return lax.dot_general(left, right, dims, preferred_element_type=F32)


def place(dp, fs):
    hi, lo = dp.bit_length() - 1, fs.bit_length() - 1
    i, f = lax.axis_index("dp"), lax.axis_index("fsdp")
    me = [(i // 2 ** (hi - 1 - t)) % 2 for t in range(hi)]
    me += [(f // 2 ** (lo - 1 - t)) % 2 for t in range(lo)]

    def partner(t):
        if t < hi:
            step = 2 ** (hi - 1 - t)
            return (i + step - 2 * step * me[t], f)
        step = 2 ** (hi + lo - 1 - t)
        return (i, f + step - 2 * step * me[t])

    return me, partner


def remote(src, dst, send, recv, device):
    return pltpu.make_async_remote_copy(
        src_ref=src, dst_ref=dst, send_sem=send, recv_sem=recv, device_id=device, device_id_type=MESH
    )


class Gather:
    def __init__(self, me, partner, order, buf, cols, send, recv):
        self.copies = []
        done = set()
        for k, t in enumerate(order):
            at = tuple(slice(None) if u in done else me[u] for u in range(len(me)))
            ref = buf.at[at + (slice(None), cols)]
            self.copies.append(remote(ref, ref, send.at[k], recv.at[k], partner(t)))
            done.add(t)

    def step(self, k):
        if k:
            self.copies[k - 1].wait_recv()
        if k < len(self.copies):
            self.copies[k].start()
        else:
            for copy in self.copies:
                copy.wait_send()


class Sum:
    def __init__(self, partner, order, held, come, send, recv):
        self.held, self.come = held, come
        self.copies = [
            remote(held.at[k], come.at[k], send.at[k], recv.at[k], partner(t))
            for k, t in enumerate(order)
        ]

    def step(self, k):
        if k:
            self.copies[k - 1].wait_recv()
            self.held[k] = self.held[k - 1] + self.come[k - 1]
        if k < len(self.copies):
            self.copies[k].start()
        else:
            for copy in self.copies:
                copy.wait_send()


class Scatter:
    def __init__(self, me, partner, order, stage, cols, come, come_cols, send, recv, finish):
        self.finish = finish
        self.copies, self.kept, self.landed = [], [], []
        left = list(range(len(me)))
        source, source_cols = stage, cols
        for k, t in enumerate(order):
            pos = left.index(t)
            every = [slice(None)] * len(left)
            keep, give = list(every), list(every)
            keep[pos], give[pos] = me[t], 1 - me[t]
            left.remove(t)
            landing = (slice(None),) * (len(left) + 1) + (come_cols,)
            self.copies.append(
                remote(
                    source.at[tuple(give) + (slice(None), source_cols)],
                    come[k].at[landing],
                    send.at[k],
                    recv.at[k],
                    partner(t),
                )
            )
            self.kept.append((source, tuple(keep) + (slice(None), source_cols)))
            self.landed.append((come[k], landing))
            source, source_cols = come[k], come_cols

    def step(self, k):
        if k:
            self.copies[k - 1].wait_recv()
            kept, kept_at = self.kept[k - 1]
            land, land_at = self.landed[k - 1]
            total = kept[kept_at].astype(F32) + land[land_at].astype(F32)
            if k < len(self.copies):
                land[land_at] = total.astype(BF16)
            else:
                self.finish(total)
        if k < len(self.copies):
            self.copies[k].start()
        else:
            for copy in self.copies:
                copy.wait_send()


ORDER = ((0, 1, 2, 3, 4), (0, 1, 3, 2, 4))
LINK = ("z", "z", "y", "x", "core")


def streams_of():
    gathers = [("vec", 0, VROWS * 512, 0)]
    gathers += [(f"q{p}", 16 * 384 * 2, 0, p % 2) for p in range(PAIRS)]
    gathers += [("o", 16 * 512 * 2, 0, 0)]
    gathers += [(f"d{i}", 64 * 256 * 2, 0, i % 2) for i in range(2)]
    gathers += [(f"u{i}", 16 * 512 * 2, 0, (i + 1) % 2) for i in range(4)]
    return gathers


def steps_of():
    steps = [("norm", 0, 3.0, [], []), ("affine", 0, 0.8, ["vec"], [])]
    steps += [("fwd", t, 2.2 + (t % 2 == 0), [f"q{t // 2}"], []) for t in range(2 * PAIRS)]
    steps += [("mid", 0, 3.0, ["o"], [])]
    for c in range(FF // CHUNK):
        steps += [("ffa", c, 7.5, ["d0", "d1", f"u{c}"], []), ("ffb", c, 2.5, [], [f"u{c}"])]
    steps[-1][4].extend(["d0", "d1"])
    steps += [("ln2", 0, 5.0, [], ["o"])]
    steps += [("bwd", t, 3.8 + (t % 2), [], [f"q{t // 2}"] if t % 2 else []) for t in range(2 * PAIRS)]
    steps += [("ln1", t, 1.6, [], ["vec"] if t == 3 else []) for t in range(4)]
    steps += [("end", 0, 0.0, ["all"], [])]
    return steps


def plan_of():
    latency = {"z": 2.2, "y": 2.2, "x": 2.2, "core": 0.8}
    rate = {"z": 45e3, "y": 45e3, "x": 45e3, "core": 250e3}
    free = dict.fromkeys(rate, 0.0)
    streams = streams_of()
    info = {name: (share, fixed, ORDER[which]) for name, share, fixed, which in streams}
    bits = len(LINK)
    pending = [("g", name, 0, 0.0) for name, *_ in streams]
    rank = {("g", s[0]): i for i, s in enumerate(streams)}
    plan = {}
    now = 0.0

    def cost(kind, name, k):
        share, fixed, order = info[name]
        bit = (order if kind == "g" else order[::-1])[k]
        size = fixed or share * 2 ** (k if kind == "g" else bits - 1 - k)
        return LINK[bit], size * (2 if bit == 0 else 1) / rate[LINK[bit]]

    def start_of(item):
        kind, name, k, ready = item
        if k == bits:
            return ready
        return max(ready, free[cost(kind, name, k)[0]])

    def issue(item, at):
        kind, name, k, ready = item
        pending.remove(item)
        if k == bits:
            return
        link, time = cost(kind, name, k)
        begin = max(at, free[link])
        free[link] = begin + time
        pending.append((kind, name, k + 1, begin + time + latency[link]))

    for name, index, time, needs, feeds in steps_of():
        taken = plan.setdefault((name, index), [])

        def open_needs():
            if "all" in needs:
                return list(pending)
            return [i for i in pending if i[0] == "g" and i[1] in needs]

        while True:
            ready = [i for i in pending if start_of(i) <= now + 0.3 and i[3] <= now]
            if ready:
                item = min(ready, key=lambda i: (start_of(i), rank.get(i[:2], 99)))
            elif open_needs():
                item = min(pending, key=lambda i: (start_of(i), rank.get(i[:2], 99)))
                now = max(now, start_of(item), item[3])
            else:
                break
            taken.append(item[:3])
            issue(item, now)
        now += time
        for fed in feeds:
            pending.append(("s", fed, 0, now))
    return plan


def norm(values):
    mean = jnp.mean(values, axis=-1, keepdims=True)
    centred = values - mean
    scale = lax.rsqrt(jnp.mean(centred * centred, axis=-1, keepdims=True) + EPS)
    return centred * scale, scale


def norm_back(grad, hat, scale, gain):
    inner = grad * gain
    return scale * (
        inner
        - jnp.mean(inner, axis=-1, keepdims=True)
        - hat * jnp.mean(inner * hat, axis=-1, keepdims=True)
    )


def gelu_both(pre):
    square = pre * pre
    tanh = jnp.tanh(pre * (GELU_A + (GELU_A * GELU_B) * square))
    half = 0.5 + 0.5 * tanh
    act = pre * half
    return act, half + act * (1.0 - tanh) * (GELU_A + (3 * GELU_A * GELU_B) * square)


def column_sum(values):
    return jnp.sum(values, axis=0, keepdims=True)


def attend_forward(qkv, mixed, lse, row0, pair):
    rows = lambda start, size: pl.ds(pl.multiple_of(row0 + start, QB), size)
    cols = lambda part: pl.ds(pl.multiple_of(pair * 384 + part * 128, 128), 128)
    out_cols = pl.ds(pl.multiple_of(pair * 128, 128), 128)
    low_all = lax.broadcasted_iota(jnp.int32, (CLIP_LEN, 128), 1) < 64
    lane = lax.broadcasted_iota(jnp.int32, (QB, 128), 1)
    low = lane < 64
    spare = lane & 63
    causal = lax.broadcasted_iota(jnp.int32, (QB, QB), 1) <= lax.broadcasted_iota(
        jnp.int32, (QB, QB), 0
    )
    one, zero = jnp.ones((), BF16), jnp.zeros((), BF16)
    queries = qkv[rows(0, CLIP_LEN), cols(0)] * jnp.asarray(HEAD_DIM**-0.5, BF16)
    keys = qkv[rows(0, CLIP_LEN), cols(1)]
    values = qkv[rows(0, CLIP_LEN), cols(2)]
    head_q = [jnp.where(low_all, queries, zero), jnp.where(low_all, zero, queries)]
    head_v = [jnp.where(low_all, values, one), jnp.where(low_all, one, values)]

    def scores(item):
        block, head = item
        n = QB * block
        s = dot(head_q[head][n : n + QB], keys[: n + QB], NT)
        diagonal = jnp.where(causal, s[:, n:], NEG)
        return jnp.concatenate([s[:, :n], diagonal], axis=1) if n else diagonal

    items = [(block, head) for block in reversed(range(CLIP_LEN // QB)) for head in range(2)]
    ahead = 3
    ready = {t: scores(items[t]) for t in range(ahead)}
    sums, tops = {}, {}
    for t, (block, head) in enumerate(items):
        s = ready.pop(t)
        top = jnp.max(s, axis=1, keepdims=True)
        if t + ahead < len(items):
            ready[t + ahead] = scores(items[t + ahead])
        weights = jnp.exp(s - top).astype(BF16)
        sums[head] = dot(weights, head_v[head][: QB * (block + 1)])
        tops[head] = top
        if head == 1:
            at = rows(QB * block, QB)
            top_sum = jnp.where(low, sums[0], sums[1])
            total = jnp.where(low, sums[1], sums[0])
            mixed[at, out_cols] = (top_sum / pltpu.roll(total, 64, 1)).astype(BF16)
            log_sum = jnp.where(low, tops[1], tops[0]) + jnp.log(total)
            high = log_sum.astype(BF16).astype(F32)
            lse[at, out_cols] = jnp.where(
                spare == 0, -high, jnp.where(spare == 1, high - log_sum, 0.0)
            ).astype(BF16)


def attend_backward(qkv, grad, lse, dots, grad_qkv, grad_qt, row0, pair):
    rows = lambda start, size: pl.ds(pl.multiple_of(row0 + start, QB), size)
    cols = lambda part: pl.ds(pl.multiple_of(pair * 384 + part * 128, 128), 128)
    one_cols = pl.ds(pl.multiple_of(pair * 128, 128), 128)
    low = lax.broadcasted_iota(jnp.int32, (CLIP_LEN, 128), 1) < 64
    causal = lax.broadcasted_iota(jnp.int32, (QB, QB), 0) <= lax.broadcasted_iota(
        jnp.int32, (QB, QB), 1
    )
    one, zero = jnp.ones((), BF16), jnp.zeros((), BF16)
    every = rows(0, CLIP_LEN)
    queries = qkv[every, cols(0)] * jnp.asarray(HEAD_DIM**-0.5, BF16)
    keys = qkv[every, cols(1)]
    values = qkv[every, cols(2)]
    out_grad = grad[every, one_cols]
    shift = lse[every, one_cols]
    row_dot = dots[every, one_cols]
    pick = lambda head, a, b: jnp.where(low, a, b) if head == 0 else jnp.where(low, b, a)
    q_shift = [pick(h, queries, shift) for h in range(2)]
    k_one = [pick(h, keys, one) for h in range(2)]
    v_one = [pick(h, values, one) for h in range(2)]
    g_shift = [pick(h, out_grad, row_dot) for h in range(2)]
    q_zero = [pick(h, queries, zero) for h in range(2)]
    g_zero = [pick(h, out_grad, zero) for h in range(2)]
    keys_t = keys.T
    items = [(block, head) for block in range(CLIP_LEN // QB) for head in range(2)]

    def products(item):
        block, head = item
        n = QB * block
        return (
            dot(k_one[head][n : n + QB], q_shift[head][n:], NT),
            dot(v_one[head][n : n + QB], g_shift[head][n:], NT),
        )

    ahead = 2
    ready = {t: products(items[t]) for t in range(ahead)}
    kept = {}
    for t, (block, head) in enumerate(items):
        n = QB * block
        s, grad_p = ready.pop(t)
        if t + ahead < len(items):
            ready[t + ahead] = products(items[t + ahead])
        probs = jnp.exp(s)
        diagonal = jnp.where(causal, probs[:, :QB], 0.0)
        probs = jnp.concatenate([diagonal, probs[:, QB:]], axis=1) if n + QB < CLIP_LEN else diagonal
        grad_s = (probs * grad_p).astype(BF16)
        kept[head] = (dot(grad_s, q_zero[head][n:]), dot(probs.astype(BF16), g_zero[head][n:]))
        half = slice(64 * head, 64 * head + 64)
        part = dot(keys_t[half, n : n + QB], grad_s)
        if block == 0:
            grad_qt[half, :] = part
        else:
            grad_qt[half, n:] = grad_qt[half, n:] + part
        if head == 1:
            at = rows(n, QB)
            grad_qkv[at, cols(1)] = (kept[0][0] + kept[1][0]).astype(BF16)
            grad_qkv[at, cols(2)] = (kept[0][1] + kept[1][1]).astype(BF16)
    grad_qkv[every, cols(0)] = (grad_qt[...].T * HEAD_DIM**-0.5).astype(BF16)


def block_kernel(dp, fs, tokens_n, linked, names, *refs):
    r = SimpleNamespace(**dict(zip(names, refs)))
    clips = tokens_n // CLIP_LEN
    tiles = tokens_n // TILE
    chunks = FF // CHUNK
    bits = len(LINK) if linked else 0
    lead = (slice(None),) * bits

    load_x = pltpu.make_async_copy(r.tokens, r.x, r.local.at[0])
    load_cot = pltpu.make_async_copy(r.cotangent, r.dy, r.local.at[1])
    load_x.start()
    load_cot.start()

    if linked:
        me, partner = place(dp, fs)
        barrier = pltpu.get_barrier_semaphore()
        for t in range(bits):
            pl.semaphore_signal(barrier, inc=1, device_id=partner(t), device_id_type=MESH)
        own = tuple(me)

        def share(flat, buf, rows, width, place_of):
            for j in range(width):
                part = flat[pl.ds(j, rows, stride=width), :].astype(BF16)
                buf[own + (slice(None), slice(128 * place_of(j), 128 * place_of(j) + 128))] = part

        per = VEC // (dp * fs)
        start = (lax.axis_index("dp") * fs + lax.axis_index("fsdp")) * per
        row, lane0 = start // 128, start % 128
        part = r.vectors[...].astype(BF16).astype(F32)
        lane = lax.broadcasted_iota(jnp.int32, (1, 128), 1)
        first = pltpu.roll(part[:, :128], lane0, 1)
        tail = jnp.concatenate([part[:, 128:], jnp.zeros((1, 256 - per), F32)], axis=1)
        second = pltpu.roll(tail, lane0, 1)
        r.vec[0] = jnp.zeros((VROWS, 128), F32)
        r.vec[0, pl.ds(row, 1), :] = jnp.where(lane >= lane0, first, 0.0)
        r.vec[0, pl.ds(row + 1, 1), :] = jnp.where(lane < lane0, first, second)
        r.vec[0, pl.ds(row + 2, 1), :] = jnp.where(lane < lane0, second, 0.0)
        share(r.qkv_weight, r.wq, 16, 12, lambda j: (j % PAIRS) * 3 + j // PAIRS)
        share(r.proj_weight, r.wo, 16, 4, lambda j: j)
        share(r.up_weight, r.w1, 16, 16, lambda j: j)
        share(r.down_weight, r.w2, 64, 4, lambda j: j)

        jobs = {}
        for n, (name, _, _, which) in enumerate(streams_of()):
            order = ORDER[which]
            gs, gr, ss, sr = r.gather_send.at[n], r.gather_recv.at[n], r.sum_send.at[n], r.sum_recv.at[n]
            kind, number = name[0], int(name[1:]) if name[1:].isdigit() else 0
            back = order[::-1]
            if name == "vec":
                jobs["g", name] = Sum(partner, order, r.vec, r.vec_come, gs, gr)
                jobs["s", name] = Sum(partner, back, r.gvec, r.gvec_come, ss, sr)
                continue
            rows, width, base, matrix, stage, come, come0 = {
                "q": (16, 384, 0, r.wq, r.sq, r.come, 0),
                "o": (16, 512, 192, r.wo, r.wo, r.come, 1536),
                "u": (16, 512, 256, r.w1, r.w1, r.come, 2048),
                "d": (64, 256, 512, r.w2, r.w2, r.come_down, 0),
            }[kind]
            cols = slice(number * width, number * width + width)
            come_cols = slice(come0 + number * width, come0 + number * width + width)

            def finish(total, kind=kind, number=number, rows=rows, width=width, base=base):
                for j in range(width // 128):
                    col = j * PAIRS + number if kind == "q" else number * (width // 128) + j
                    stride = {"q": 12, "o": 4, "u": 16, "d": 4}[kind]
                    r.total[pl.ds(base + col, rows, stride=stride), :] = total[:, 128 * j : 128 * j + 128]

            jobs["g", name] = Gather(me, partner, order, matrix, cols, gs, gr)
            jobs["s", name] = Scatter(
                me, partner, back, stage, cols, come, come_cols, ss, sr, finish
            )
        plan = plan_of()
        pl.semaphore_wait(barrier, bits)
    else:
        loads = [
            pltpu.make_async_copy(src, dst, r.local.at[3 + n])
            for n, (src, dst) in enumerate(
                [(r.qkv_mat, r.wq), (r.proj_mat, r.wo), (r.up_mat, r.w1), (r.down_mat, r.w2)]
            )
        ]
        for load in loads:
            load.start()
        r.vec[0] = r.vec_in[...]
        for load in loads:
            load.wait()

    def exchange(name, index):
        if not linked:
            return
        for (step, at), taken in plan.items():
            if step != name or not taken:
                continue

            def act(taken=taken):
                for kind, stream, k in taken:
                    jobs[kind, stream].step(k)

            if isinstance(index, int):
                if index == at:
                    act()
            else:
                pl.when(index == at)(act)

    vec = r.vec.at[bits]
    gvec = r.gvec.at[0]
    gvec[...] = jnp.zeros((VROWS, 128), F32)

    def vector(first, count):
        return jnp.concatenate([vec[first + n : first + n + 1, :] for n in range(count)], axis=1)

    def add_vector(first, values):
        for n in range(values.shape[1] // 128):
            gvec[first + n : first + n + 1, :] += values[:, 128 * n : 128 * n + 128]

    def whole(ref, cols):
        got = ref[lead + (slice(None), cols)]
        return got.reshape(-1, got.shape[-1])

    def down_chunk(c):
        if linked:
            return r.w2[c // 2, c % 2].reshape(CHUNK, D)
        return r.w2[pl.ds(pl.multiple_of(c * CHUNK, CHUNK), CHUNK), :]

    rows_of = lambda i, size: pl.ds(pl.multiple_of(i * size, size), size)
    act = lambda rows: r.big.at[rows, pl.ds(0, 512)]
    grad_pre = lambda rows: r.big.at[rows, pl.ds(512, 512)]
    normed_two = lambda rows: r.big.at[rows, pl.ds(1024, 512)]
    everything = pl.ds(0, tokens_n)

    exchange("norm", 0)
    load_x.wait()

    def norm_one(i, carry):
        rows = rows_of(i, 256)
        r.hat[rows, :] = norm(r.x[rows, :].astype(F32))[0]
        return carry

    lax.fori_loop(0, tokens_n // 256, norm_one, 0)
    exchange("affine", 0)

    def affine_one(i, carry):
        rows = rows_of(i, 256)
        r.a[rows, :] = (r.hat[rows, :] * vector(G1, 4) + vector(S1, 4)).astype(BF16)
        return carry

    lax.fori_loop(0, tokens_n // 256, affine_one, 0)

    def forward(t, carry):
        exchange("fwd", t)
        pair, clip = t // clips, t % clips

        @pl.when(clip == 0)
        def _():
            cols = pl.ds(pl.multiple_of(pair * 384, 128), 384)
            matrix = whole(r.wq, cols)
            bias = jnp.concatenate([vec[pl.ds(BQKV + 4 * n + pair, 1), :] for n in range(3)], axis=1)
            for i in range(tiles):
                rows = slice(i * TILE, i * TILE + TILE)
                r.qkv[rows, cols] = (dot(r.a[rows, :], matrix) + bias).astype(BF16)

        attend_forward(r.qkv, r.mixed, r.lse, clip * CLIP_LEN, pair)
        return carry

    lax.fori_loop(0, PAIRS * clips, forward, 0)

    exchange("mid", 0)
    load_cot.wait()

    def middle(i, carry):
        rows = rows_of(i, TILE)
        h = r.x[rows, :].astype(F32) + dot(r.mixed[rows, :], whole(r.wo, slice(None))) + vector(BO, 4)
        hat, scale = norm(h)
        r.hat[rows, :] = hat
        r.scale[rows, :] = jnp.broadcast_to(scale, (TILE, 128))
        normed_two(rows)[...] = (hat * vector(G2, 4) + vector(S2, 4)).astype(BF16)
        r.total_out[rows, :] = h + vector(B2, 4)
        r.grad_h[rows, :] = jnp.zeros((TILE, D), F32)
        per = CLIP_LEN // TILE
        place_in = (i % per) * TILE + lax.broadcasted_iota(jnp.int32, (TILE, 1), 0)
        dy = jnp.where(place_in >= r.cond_frames[i // per] * FRAME_TOK, r.dy[rows, :].astype(F32), 0.0)
        add_vector(B2, column_sum(dy))
        r.dy[rows, :] = dy.astype(BF16)
        return carry

    lax.fori_loop(0, tiles, middle, 0)

    def feed(c, carry):
        exchange("ffa", c)
        cols = pl.ds(pl.multiple_of(c * CHUNK, CHUNK), CHUNK)
        up, down = whole(r.w1, cols), down_chunk(c)
        bias = jnp.concatenate([vec[pl.ds(B1 + 4 * c + n, 1), :] for n in range(4)], axis=1)
        spans = [slice(i * TILE, i * TILE + TILE) for i in range(tiles)]

        def products(rows):
            return dot(normed_two(rows)[...], up), dot(r.dy[rows, :], down, NT)

        ready = products(spans[0])
        bias_grad = jnp.zeros((1, CHUNK), F32)
        for i, rows in enumerate(spans):
            pre, grad_act = ready
            if i + 1 < tiles:
                ready = products(spans[i + 1])
            value, slope = gelu_both(pre + bias)
            value = value.astype(BF16)
            grad = (slope * grad_act).astype(BF16)
            bias_grad = bias_grad + column_sum(grad.astype(F32))
            act(rows)[...] = value
            grad_pre(rows)[...] = grad
            r.total_out[rows, :] += dot(value, down)
            r.grad_h[rows, :] += dot(grad, up, NT)
        for n in range(4):
            gvec[pl.ds(B1 + 4 * c + n, 1), :] = bias_grad[:, 128 * n : 128 * n + 128]
        exchange("ffb", c)
        grad_up = dot(normed_two(everything)[...], grad_pre(everything)[...], TN).astype(BF16)
        grad_down = dot(act(everything)[...], r.dy[...], TN).astype(BF16)
        if linked:
            r.w1[lead + (slice(None), cols)] = grad_up.reshape((2,) * bits + (16, CHUNK))
            r.w2[c // 2, c % 2] = grad_down.reshape((2,) * (bits - 2) + (64, D))
        else:
            r.w1[:, cols] = grad_up
            r.w2[rows_of(c, CHUNK), :] = grad_down
        return carry

    lax.fori_loop(0, chunks, feed, 0)

    exchange("ln2", 0)
    ri = lax.broadcasted_iota(jnp.int32, (128, 128), 0)
    ci = lax.broadcasted_iota(jnp.int32, (128, 128), 1)
    other_half = jnp.where((ri < 64) != (ci < 64), 1.0, 0.0).astype(BF16)
    spare = lax.broadcasted_iota(jnp.int32, (TILE, 128), 1) & 63
    proj = whole(r.wo, slice(None))
    grad_proj = jnp.zeros((D, D), F32)
    for i in range(tiles):
        rows = slice(i * TILE, i * TILE + TILE)
        r.out_low[rows, :] = r.total_out[rows, :].astype(BF16)
        grad, hat, scale = r.grad_h[rows, :], r.hat[rows, :], r.scale[rows, :1]
        add_vector(G2, column_sum(grad * hat))
        add_vector(S2, column_sum(grad))
        grad = r.dy[rows, :].astype(F32) + norm_back(grad, hat, scale, vector(G2, 4))
        r.grad_h[rows, :] = grad
        low = grad.astype(BF16)
        add_vector(BO, column_sum(low.astype(F32)))
        mixed = r.mixed[rows, :]
        grad_proj = grad_proj + dot(mixed, low, TN)
        grad_mixed = dot(low, proj, NT).astype(BF16)
        r.dy[rows, :] = grad_mixed
        product = grad_mixed.astype(F32) * mixed.astype(F32)
        high = product.astype(BF16)
        rest = (product - high.astype(F32)).astype(BF16)
        for p in range(PAIRS):
            cols = slice(128 * p, 128 * p + 128)
            row_dot = dot(high[:, cols], other_half) + dot(rest[:, cols], other_half)
            top = row_dot.astype(BF16).astype(F32)
            r.mixed[rows, cols] = jnp.where(
                spare == 0, -top, jnp.where(spare == 1, top - row_dot, 0.0)
            ).astype(BF16)
    grad_proj = grad_proj.astype(BF16)
    if linked:
        r.wo[...] = grad_proj.reshape((2,) * bits + (16, D))
    else:
        r.wo[...] = grad_proj
    store_out = pltpu.make_async_copy(r.out_low, r.output, r.local.at[2])
    store_out.start()

    def backward(t, carry):
        exchange("bwd", t)
        pair, clip = t // clips, t % clips
        attend_backward(r.qkv, r.dy, r.lse, r.mixed, r.big, r.grad_qt, clip * CLIP_LEN, pair)

        @pl.when(clip == clips - 1)
        def _():
            cols = pl.ds(pl.multiple_of(pair * 384, 128), 384)
            grad = r.big[:, cols]
            sums = column_sum(grad.astype(F32))
            for n in range(3):
                gvec[pl.ds(BQKV + 4 * n + pair, 1), :] = sums[:, 128 * n : 128 * n + 128]
            matrix = dot(r.a[...], grad, TN).astype(BF16)
            if linked:
                r.sq[lead + (slice(None), cols)] = matrix.reshape((2,) * bits + (16, 384))
            else:
                r.sq[:, cols] = matrix

        return carry

    lax.fori_loop(0, PAIRS * clips, backward, 0)

    def first_back(i, carry):
        exchange("ln1", i)
        rows = rows_of(i, TILE)
        grad = dot(r.big[rows, :], whole(r.wq, slice(None)), NT)
        hat, scale = norm(r.x[rows, :].astype(F32))
        add_vector(G1, column_sum(grad * hat))
        add_vector(S1, column_sum(grad))
        r.grad_h[rows, :] += norm_back(grad, hat, scale, vector(G1, 4))
        return carry

    lax.fori_loop(0, tiles, first_back, 0)
    store_grad = pltpu.make_async_copy(r.grad_h, r.input_grad, r.local.at[3])
    store_grad.start()
    exchange("end", 0)
    if linked:
        r.total_vec[...] = r.gvec[bits]
    else:
        stores = [
            pltpu.make_async_copy(src, dst, r.local.at[4 + n])
            for n, (src, dst) in enumerate(
                [(r.sq, r.qkv_grad), (r.wo, r.proj_grad), (r.w1, r.up_grad), (r.w2, r.down_grad)]
            )
        ]
        for store in stores:
            store.start()
        for store in stores:
            store.wait()
        r.total_vec[...] = gvec[...]
    store_out.wait()
    store_grad.wait()


def run_block(dp, fs, linked, tokens, cotangent, cond_frames, weights):
    n = tokens.shape[0]
    shape = jax.ShapeDtypeStruct
    vmem, smem, any_ = (
        pl.BlockSpec(memory_space=pltpu.VMEM),
        pl.BlockSpec(memory_space=pltpu.SMEM),
        pl.BlockSpec(memory_space=pl.ANY),
    )
    bits = len(LINK) if linked else 0
    ins = ["tokens", "cotangent", "cond_frames"]
    in_specs = [any_, any_, smem]
    outs = {"output": ((n, D), BF16, any_), "input_grad": ((n, D), F32, any_)}
    outs["total_vec"] = ((VROWS, 128), F32, vmem)
    if linked:
        ins += ["qkv_weight", "proj_weight", "up_weight", "down_weight", "vectors"]
        in_specs += [vmem] * 5
        outs["total"] = ((768, 128), F32, vmem)
        matrix = lambda rows, cols: pltpu.VMEM((2,) * bits + (rows // 2**bits, cols), BF16)
    else:
        ins += ["qkv_mat", "proj_mat", "up_mat", "down_mat", "vec_in"]
        in_specs += [any_] * 4 + [vmem]
        outs["qkv_grad"] = ((D, 3 * D), BF16, any_)
        outs["proj_grad"] = ((D, D), BF16, any_)
        outs["up_grad"] = ((D, FF), BF16, any_)
        outs["down_grad"] = ((FF, D), BF16, any_)
        matrix = lambda rows, cols: pltpu.VMEM((rows, cols), BF16)
    scratch = {
        "x": pltpu.VMEM((n, D), BF16),
        "a": pltpu.VMEM((n, D), BF16),
        "dy": pltpu.VMEM((n, D), BF16),
        "qkv": pltpu.VMEM((n, 3 * D), BF16),
        "mixed": pltpu.VMEM((n, D), BF16),
        "lse": pltpu.VMEM((n, D), BF16),
        "hat": pltpu.VMEM((n, D), F32),
        "total_out": pltpu.VMEM((n, D), F32),
        "grad_h": pltpu.VMEM((n, D), F32),
        "scale": pltpu.VMEM((n, 128), F32),
        "big": pltpu.VMEM((n, 3 * D), BF16),
        "out_low": pltpu.VMEM((n, D), BF16),
        "grad_qt": pltpu.VMEM((128, CLIP_LEN), F32),
        "wq": matrix(D, 3 * D),
        "sq": matrix(D, 3 * D),
        "wo": matrix(D, D),
        "w1": matrix(D, FF),
        "w2": matrix(FF, D),
        "vec": pltpu.VMEM((bits + 1, VROWS, 128), F32),
        "gvec": pltpu.VMEM((bits + 1, VROWS, 128), F32),
        "local": pltpu.SemaphoreType.DMA((8,)),
    }
    names = ins + list(outs) + list(scratch)
    shapes = list(scratch.values())
    if linked:
        count = len(streams_of())
        for name in ("vec_come", "gvec_come"):
            names.append(name)
            shapes.append(pltpu.VMEM((bits, VROWS, 128), F32))
        for name in ("gather_send", "gather_recv", "sum_send", "sum_recv"):
            names.append(name)
            shapes.append(pltpu.SemaphoreType.DMA((count, bits)))
        for k in range(bits):
            names.append(f"come{k}")
            shapes.append(pltpu.VMEM((2,) * (bits - 1 - k) + (16, 8 * D), BF16))
        for k in range(bits):
            names.append(f"come_down{k}")
            shapes.append(pltpu.VMEM((2,) * (bits - 1 - k) + (64, D), BF16))

    def body(*refs):
        table = dict(zip(names, refs))
        if linked:
            table["come"] = [table.pop(f"come{k}") for k in range(bits)]
            table["come_down"] = [table.pop(f"come_down{k}") for k in range(bits)]
        block_kernel(dp, fs, n, linked, list(table), *table.values())

    params = dict(vmem_limit_bytes=64 << 20)
    if linked:
        params.update(collective_id=0, has_side_effects=True)
    return pl.pallas_call(
        body,
        out_shape=[shape(s, t) for s, t, _ in outs.values()],
        in_specs=in_specs,
        out_specs=[spec for *_, spec in outs.values()],
        scratch_shapes=shapes,
        compiler_params=pltpu.CompilerParams(**params),
        name="block",
    )(tokens, cotangent, cond_frames, *weights)


def adamw(weight, grad, first, second, average, rate, decay):
    first_new = BETA_ONE * first + (1.0 - BETA_ONE) * grad
    second_new = BETA_TWO * second + (1.0 - BETA_TWO) * grad * grad
    first_hat = first_new / (1.0 - BETA_ONE**STEP)
    second_hat = second_new / (1.0 - BETA_TWO**STEP)
    weight_new = weight - rate * (first_hat / (jnp.sqrt(second_hat) + ADAM_EPS) + decay * weight)
    average_new = EMA_KEEP * average + (1.0 - EMA_KEEP) * weight_new
    return (first_new, second_new, weight_new, average_new)


def adam_kernel(dp, fs, *refs):
    total, total_vec = refs[:2]
    ins, outs = refs[2:22], refs[22:]
    base = 0
    for m in range(4):
        weight, first, second, average = ins[4 * m : 4 * m + 4]
        size = weight.shape[0]
        new = adamw(
            weight[...], total[base : base + size, :], first[...], second[...], average[...],
            RATE_MATRIX, WEIGHT_DECAY,
        )
        for ref, value in zip(outs[4 * m : 4 * m + 4], new):
            ref[...] = value
        base += size
    per = VEC // (dp * fs)
    start = (lax.axis_index("dp") * fs + lax.axis_index("fsdp")) * per
    row, lane0 = start // 128, start % 128
    lane = lax.broadcasted_iota(jnp.int32, (1, 128), 1)
    back = lax.rem(128 - lane0, 128)
    parts = [pltpu.roll(total_vec[pl.ds(row + n, 1), :], back, 1) for n in range(3)]
    keep = 128 - lane0
    grad = jnp.concatenate(
        [jnp.where(lane < keep, parts[0], parts[1]), jnp.where(lane < keep, parts[1], parts[2])], axis=1
    )[:, :per]
    weight, first, second, average = ins[16:]
    new = adamw(
        weight[...], grad, first[...], second[...], average[...], RATE_VECTOR, 0.0
    )
    for ref, value in zip(outs[16:], new):
        ref[...] = value


def run_adam(dp, fs, total, total_vec, state):
    flat = [a.reshape(-1, 128) for a in state[:16]] + list(state[16:])
    vmem = pl.BlockSpec(memory_space=pltpu.VMEM)
    new = pl.pallas_call(
        functools.partial(adam_kernel, dp, fs),
        out_shape=[jax.ShapeDtypeStruct(a.shape, F32) for a in flat],
        in_specs=[vmem] * 22,
        out_specs=[vmem] * 20,
        compiler_params=pltpu.CompilerParams(vmem_limit_bytes=64 << 20),
        name="adam",
    )(total, total_vec, *flat)
    return [a.reshape(b.shape) for a, b in zip(new, state)]


def local(dp, fs, tokens, cotangent, cond_frames, *state):
    weights, firsts, seconds, averages = (state[5 * n : 5 * n + 5] for n in range(4))
    shards = dp * fs
    linked = shards == 2 ** len(LINK) and not (dp & (dp - 1))
    if linked:
        shares = [w.reshape(-1, 128) for w in weights[:4]] + [weights[4]]
        output, input_grad, total_vec, total = run_block(
            dp, fs, True, tokens, cotangent, cond_frames, shares
        )
    else:
        gathered = [
            lax.all_gather(w.astype(BF16), AXES, axis=0, tiled=True) for w in weights
        ]
        qkv = gathered[0].reshape(D, 3, PAIRS, 128).swapaxes(1, 2).reshape(D, 3 * D)
        vec = jnp.pad(gathered[4].astype(F32).reshape(-1, 128), ((0, VROWS - VEC // 128), (0, 0)))
        mats = [qkv] + [g.reshape(-1, c) for g, c in zip(gathered[1:4], (D, FF, D))] + [vec]
        output, input_grad, total_vec, *grads = run_block(
            dp, fs, False, tokens, cotangent, cond_frames, mats
        )
        grads[0] = grads[0].reshape(D, PAIRS, 3, 128).swapaxes(1, 2).reshape(D, 3 * D)
        scatter = lambda g: lax.psum_scatter(
            g.astype(F32).reshape(shards, -1), AXES, scatter_dimension=0, tiled=True
        )
        total = jnp.concatenate([scatter(g).reshape(-1, 128) for g in grads], axis=0)
        total_vec = lax.psum(total_vec, AXES)
    order = [group[m] for m in range(5) for group in (weights, firsts, seconds, averages)]
    new = run_adam(dp, fs, total, total_vec, order)
    return (output, input_grad, *new)


def solution(mesh):
    dp, fs = mesh.shape["dp"], mesh.shape["fsdp"]
    split = P(AXES, None)
    return jax.shard_map(
        functools.partial(local, dp, fs),
        mesh=mesh,
        in_specs=(split, split, P(AXES)) + (split,) * 20,
        out_specs=(split,) * 22,
        check_vma=False,
    )
```

time: 697 us -> 158 us (0.23)
  matrix products: 193 us -> 0 us
  Pallas kernels: 0 us -> 152 us
  waiting for transfers between devices: 140 us -> 0 us
  blocking collectives: 122 us -> 0 us
  other arithmetic: 117 us -> 0 us
  local copies, waits for them, and re-layouts: 104 us -> 5.22 us
  between operations: 14.9 us -> 0.68 us
    dot_general x40 -> x0, matrix products: 193 us -> none  [the longest x4 23.9 us: attend_backward(): jnp.einsum('qhd,khd->hqk', go_block, values_part[:stop], preferred_elemen...]
    pallas_call x0 -> x2, Pallas kernels: none -> 152 us  [the longest x1 149 us: run_block(): pl.pallas_call(body, out_shape=[shape(s, t) for s, t, _ in outs.values()]...]
    unnamed x5 -> x0, waiting for transfers between devices: 140 us -> none
    all_gather x2 -> x0, blocking collectives: 84.3 us -> none  [the longest x1 43.2 us: local(): lax.all_gather(vectors.astype(jnp.bfloat16), ('dp', 'fsdp'), axis=0, tile...]
    all_gather x4 -> x0, other arithmetic: 40.5 us -> none  [the longest x1 12.5 us: local(): lax.all_gather(up_weight.astype(jnp.bfloat16), ('dp', 'fsdp'), axis=0, ti...]
    unnamed x1 -> x0, blocking collectives: 37.3 us -> none
    reduce_sum x14 -> x0, other arithmetic: 35 us -> none  [the longest x4 12.2 us: attend_forward(): total = jnp.sum(exponent, axis=-1, keepdims=True)]
    while x58 -> x0, local copies, waits for them, and re-layouts: 24.1 us -> none  [the longest x1 8.79 us: local(): lax.map(attend_backward, (qkv_clips, grad_att.reshape(clips, CLIP_LEN, D)...]
  transfers between devices with their start and end apart: 4 -> 0, of which waited for: 1 -> 0; matrix products, arithmetic and copies ran while one was open for 24% -> 0% of each run, Pallas kernels for 0% -> 0%
where the time goes in v1:
time: 158 us
  Pallas kernels  152 us (96%)
  local copies, waits for them, and re-layouts  5.22 us (3%)
    pallas_call x1, Pallas kernels, run_block(): pl.pallas_call(body, out_shape=[shape(s, t) for s, t, _ in outs.values()]...  149 us
    unnamed x4, local copies, waits for them, and re-layouts  5.22 us

profile of v1, /device:TPU:0, one launch (start us, length us, event | category | flops | bytes accessed | tf_op | source)
XLA Modules:
  0.0 157.6 jit_solution(7687209834825340088)
XLA Ops:
  0.7 148.7 %block.1 = (bf16[2048,512]{1,0:T(8,128)(2,1)}, f32[2048,512]{1,0:T(8,128)}, f32[56,128]{1,0:T(8,128)}, f32[768,128]{1,0:T(8,128)}) custom-call(bf16[2048,512]{1,0:T(8,128)(2,1)} %refs_0_.1, bf16[2048,512]{1,0:T(8,128)(2,1)} %refs_1_.1, s32[2]{0:T(128)} %refs_2_.1, f32[192,128]{1,0:T(8,128)} %bitcast.36, f32[64,128]{1,0:T(8,128)} %bitcast.38, ...), custom_call_target="tpu_custom_call" | custom-call | tf_op jit(solution)/shard_map/block/pallas_call | solution.py:772
  149.4 3.0 %adam.1 = (f32[192,128]{1,0:T(8,128)}, f32[192,128]{1,0:T(8,128)}, f32[192,128]{1,0:T(8,128)}, f32[192,128]{1,0:T(8,128)}, f32[64,128]{1,0:T(8,128)}, /*index=5*...) custom-call(f32[768,128]{1,0:T(8,128)} %get-tuple-element.48.refs_0_, ...), custom_call_target="tpu_custom_call" | custom-call | tf_op jit(solution)/shard_map/adam/pallas_call | solution.py:828
  152.3 0.0 copy-start
  152.3 3.2 %copy.47 = bf16[2048,512]{1,0:T(8,128)(2,1)} copy(bf16[2048,512]{1,0:T(8,128)(2,1)} %get-tuple-element.92) | data formatting | bytes 4194304
  155.5 0.0 copy-done
  155.6 2.0 %copy.48 = f32[2048,512]{1,0:T(8,128)} copy(f32[2048,512]{1,0:T(8,128)S(1)} %copy-done) | data formatting | bytes 8388608
Async XLA Ops:
  152.3 3.2 %copy-start = (f32[2048,512]{1,0:T(8,128)S(1)}, f32[2048,512]{1,0:T(8,128)}, u32[]{:S(2)}) copy-start(f32[2048,512]{1,0:T(8,128)} %get-tuple-element.93) | copy-start | bytes 12582916

commit v2 on v1

--- a/solution.py
+++ b/solution.py
@@ -48,18 +48,31 @@
     return lax.dot_general(left, right, dims, preferred_element_type=F32)
 
 
+BITS = 5
+Z, Y, X, XY, CORE = (0, 1), (2,), (3,), (2, 3), (4,)
+LINK = {0: "z", 1: "z", 2: "y", 3: "x", 4: "core"}
+
+
+def masks_of(hop):
+    return [(hop[0],)] if len(hop) == 1 else [(hop[1],), (hop[0],), hop]
+
+
 def place(dp, fs):
     hi, lo = dp.bit_length() - 1, fs.bit_length() - 1
     i, f = lax.axis_index("dp"), lax.axis_index("fsdp")
     me = [(i // 2 ** (hi - 1 - t)) % 2 for t in range(hi)]
     me += [(f // 2 ** (lo - 1 - t)) % 2 for t in range(lo)]
 
-    def partner(t):
-        if t < hi:
-            step = 2 ** (hi - 1 - t)
-            return (i + step - 2 * step * me[t], f)
-        step = 2 ** (hi + lo - 1 - t)
-        return (i, f + step - 2 * step * me[t])
+    def partner(mask):
+        at_i, at_f = i, f
+        for t in mask:
+            if t < hi:
+                step = 2 ** (hi - 1 - t)
+                at_i = at_i + step - 2 * step * me[t]
+            else:
+                step = 2 ** (hi + lo - 1 - t)
+                at_f = at_f + step - 2 * step * me[t]
+        return (at_i, at_f)
 
     return me, partner
 
@@ -70,172 +83,180 @@
     )
 
 
-class Gather:
-    def __init__(self, me, partner, order, buf, cols, send, recv):
-        self.copies = []
-        done = set()
-        for k, t in enumerate(order):
-            at = tuple(slice(None) if u in done else me[u] for u in range(len(me)))
-            ref = buf.at[at + (slice(None), cols)]
-            self.copies.append(remote(ref, ref, send.at[k], recv.at[k], partner(t)))
-            done.add(t)
-
+def split_bits(n):
+    return tuple(n >> (BITS - 1 - t) & 1 for t in range(BITS))
+
+
+class Transfer:
     def step(self, k):
         if k:
-            self.copies[k - 1].wait_recv()
-        if k < len(self.copies):
-            self.copies[k].start()
+            for copy in self.hops[k - 1]:
+                copy.wait_recv()
+            self.arrived(k - 1)
+        if k < len(self.hops):
+            for copy in self.hops[k]:
+                copy.start()
         else:
-            for copy in self.copies:
-                copy.wait_send()
-
-
-class Sum:
-    def __init__(self, partner, order, held, come, send, recv):
-        self.held, self.come = held, come
-        self.copies = [
-            remote(held.at[k], come.at[k], send.at[k], recv.at[k], partner(t))
-            for k, t in enumerate(order)
-        ]
-
-    def step(self, k):
-        if k:
-            self.copies[k - 1].wait_recv()
-            self.held[k] = self.held[k - 1] + self.come[k - 1]
-        if k < len(self.copies):
-            self.copies[k].start()
+            for hop in self.hops:
+                for copy in hop:
+                    copy.wait_send()
+
+    def arrived(self, k):
+        pass
+
+
+class Gather(Transfer):
+    def __init__(self, me, partner, hops, left, buf, cols, send, recv):
+        self.hops = []
+        done, n = set(), 0
+        for hop in hops:
+            at = tuple(slice(None) if t in done else me[t] for t in left)
+            ref = buf.at[at + (slice(None), cols)]
+            copies = []
+            for mask in masks_of(hop):
+                copies.append(remote(ref, ref, send(n), recv(n), partner(mask)))
+                n += 1
+            self.hops.append(copies)
+            done.update(hop)
+
+
+class Scatter(Transfer):
+    def __init__(self, me, partner, hops, left, stage, cols, come, send, recv, finish):
+        self.hops, self.sums = [], []
+        self.finish = finish
+        left, n = list(left), 0
+        source, source_cols = stage, cols
+        for k, hop in enumerate(hops):
+
+            def part(mask):
+                at = [(1 - me[t] if t in mask else me[t]) if t in hop else slice(None) for t in left]
+                return tuple(at) + (slice(None), source_cols)
+
+            copies = []
+            for slot, mask in enumerate(masks_of(hop)):
+                copies.append(
+                    remote(source.at[part(mask)], come[k].at[slot], send(n), recv(n), partner(mask))
+                )
+                n += 1
+            self.hops.append(copies)
+            self.sums.append((source, part(()), come[k], len(copies)))
+            left = [t for t in left if t not in hop]
+            source, source_cols = come[k].at[0], slice(None)
+
+    def arrived(self, k):
+        source, at, come, count = self.sums[k]
+        total = source[at].astype(F32)
+        for slot in range(count):
+            total = total + come[slot].astype(F32)
+        if k + 1 < len(self.hops):
+            come[0] = total.astype(come.dtype)
         else:
-            for copy in self.copies:
-                copy.wait_send()
-
-
-class Scatter:
-    def __init__(self, me, partner, order, stage, cols, come, come_cols, send, recv, finish):
-        self.finish = finish
-        self.copies, self.kept, self.landed = [], [], []
-        left = list(range(len(me)))
-        source, source_cols = stage, cols
-        for k, t in enumerate(order):
-            pos = left.index(t)
-            every = [slice(None)] * len(left)
-            keep, give = list(every), list(every)
-            keep[pos], give[pos] = me[t], 1 - me[t]
-            left.remove(t)
-            landing = (slice(None),) * (len(left) + 1) + (come_cols,)
-            self.copies.append(
-                remote(
-                    source.at[tuple(give) + (slice(None), source_cols)],
-                    come[k].at[landing],
-                    send.at[k],
-                    recv.at[k],
-                    partner(t),
-                )
-            )
-            self.kept.append((source, tuple(keep) + (slice(None), source_cols)))
-            self.landed.append((come[k], landing))
-            source, source_cols = come[k], come_cols
-
-    def step(self, k):
-        if k:
-            self.copies[k - 1].wait_recv()
-            kept, kept_at = self.kept[k - 1]
-            land, land_at = self.landed[k - 1]
-            total = kept[kept_at].astype(F32) + land[land_at].astype(F32)
-            if k < len(self.copies):
-                land[land_at] = total.astype(BF16)
-            else:
-                self.finish(total)
-        if k < len(self.copies):
-            self.copies[k].start()
-        else:
-            for copy in self.copies:
-                copy.wait_send()
-
-
-ORDER = ((0, 1, 2, 3, 4), (0, 1, 3, 2, 4))
-LINK = ("z", "z", "y", "x", "core")
+            self.finish(total)
 
 
 def streams_of():
-    gathers = [("vec", 0, VROWS * 512, 0)]
-    gathers += [(f"q{p}", 16 * 384 * 2, 0, p % 2) for p in range(PAIRS)]
-    gathers += [("o", 16 * 512 * 2, 0, 0)]
-    gathers += [(f"d{i}", 64 * 256 * 2, 0, i % 2) for i in range(2)]
-    gathers += [(f"u{i}", 16 * 512 * 2, 0, (i + 1) % 2) for i in range(4)]
-    return gathers
+    first, second = (Z, Y, X, CORE), (Z, X, Y, CORE)
+    every = (0, 1, 2, 3, 4)
+    streams = {"vec": ((Z, XY, CORE), every, 8, 128, 4)}
+    for p in range(PAIRS):
+        hops = (Z, XY, CORE) if p in (0, PAIRS - 1) else (first, second)[p % 2]
+        streams[f"q{p}"] = (hops, every, 16, 384, 2)
+    streams["o"] = (first, every, 16, 512, 2)
+    streams["u0"] = (second, every, 16, 512, 2)
+    streams["dz"] = ((Z,), every, 64, 512, 2)
+    streams["d0"] = (first[1:], every[2:], 64, 512, 2)
+    for c in range(1, FF // CHUNK):
+        streams[f"u{c}"] = ((second, first)[c % 2], every, 16, 512, 2)
+        streams[f"d{c}"] = ((first, second)[c % 2][1:], every[2:], 64, 512, 2)
+    return streams
 
 
 def steps_of():
     steps = [("norm", 0, 3.0, [], []), ("affine", 0, 0.8, ["vec"], [])]
-    steps += [("fwd", t, 2.2 + (t % 2 == 0), [f"q{t // 2}"], []) for t in range(2 * PAIRS)]
+    steps += [("fwd", t, 2.0 + (t % 2 == 0), [f"q{t // 2}"], []) for t in range(2 * PAIRS)]
     steps += [("mid", 0, 3.0, ["o"], [])]
     for c in range(FF // CHUNK):
-        steps += [("ffa", c, 7.5, ["d0", "d1", f"u{c}"], []), ("ffb", c, 2.5, [], [f"u{c}"])]
-    steps[-1][4].extend(["d0", "d1"])
+        steps += [("ffa", c, 7.5, ["dz", f"d{c}", f"u{c}"], []), ("ffb", c, 2.5, [], [f"u{c}", f"d{c}"])]
     steps += [("ln2", 0, 5.0, [], ["o"])]
-    steps += [("bwd", t, 3.8 + (t % 2), [], [f"q{t // 2}"] if t % 2 else []) for t in range(2 * PAIRS)]
-    steps += [("ln1", t, 1.6, [], ["vec"] if t == 3 else []) for t in range(4)]
+    steps += [("bwd", t, 3.5 + (t % 2), [], [f"q{t // 2}"] if t % 2 else []) for t in range(2 * PAIRS)]
+    steps += [("sums", t, 1.0, [], ["vec"] if t == 3 else []) for t in range(4)]
+    steps += [("ln1", t, 0.6, [], []) for t in range(4)]
     steps += [("end", 0, 0.0, ["all"], [])]
     return steps
 
 
 def plan_of():
-    latency = {"z": 2.2, "y": 2.2, "x": 2.2, "core": 0.8}
+    latency = {"z": 2.0, "y": 2.0, "x": 2.0, "core": 0.8}
     rate = {"z": 45e3, "y": 45e3, "x": 45e3, "core": 250e3}
     free = dict.fromkeys(rate, 0.0)
     streams = streams_of()
-    info = {name: (share, fixed, ORDER[which]) for name, share, fixed, which in streams}
-    bits = len(LINK)
-    pending = [("g", name, 0, 0.0) for name, *_ in streams]
-    rank = {("g", s[0]): i for i, s in enumerate(streams)}
-    plan = {}
+    rank = {("g", s): n for n, s in enumerate(streams)}
+    rank.update({("s", s): 50 + n for n, s in enumerate(streams)})
+    rank["s", f"q{PAIRS - 1}"], rank["s", "vec"] = 1, 0
+    arrived = {}
+    after = {("g", f"d{c}"): [("g", "dz")] for c in range(4)}
+    after["s", "dz"] = [("s", f"d{c}") for c in range(4)]
+    pending = [("g", s, 0, 0.0) for s in streams if ("g", s) not in after]
+    plan, model = {}, []
     now = 0.0
 
     def cost(kind, name, k):
-        share, fixed, order = info[name]
-        bit = (order if kind == "g" else order[::-1])[k]
-        size = fixed or share * 2 ** (k if kind == "g" else bits - 1 - k)
-        return LINK[bit], size * (2 if bit == 0 else 1) / rate[LINK[bit]]
+        hops, bits, rows, cols, size = streams[name]
+        hop = (hops if kind == "g" else hops[::-1])[k]
+        done = [t for h in (hops[:k] if kind == "g" else hops[: len(hops) - 1 - k]) for t in h]
+        held = rows * cols * size * 2 ** len(done)
+        if hop == Z:
+            return {"z": 4 * held / rate["z"]}
+        if hop == XY:
+            return {"x": 2 * held / rate["x"], "y": 2 * held / rate["y"]}
+        return {LINK[hop[0]]: held / rate[LINK[hop[0]]]}
 
     def start_of(item):
         kind, name, k, ready = item
-        if k == bits:
+        if k == len(streams[name][0]):
             return ready
-        return max(ready, free[cost(kind, name, k)[0]])
+        return max([ready] + [free[link] for link in cost(kind, name, k)])
 
     def issue(item, at):
         kind, name, k, ready = item
         pending.remove(item)
-        if k == bits:
+        if k == len(streams[name][0]):
+            arrived[kind, name] = max(at, ready)
+            for other, needs in after.items():
+                if (kind, name) in needs and all(n in arrived for n in needs):
+                    pending.append((*other, 0, max(at, ready)))
             return
-        link, time = cost(kind, name, k)
-        begin = max(at, free[link])
-        free[link] = begin + time
-        pending.append((kind, name, k + 1, begin + time + latency[link]))
+        begin, end = max(at, start_of(item)), 0.0
+        for link, time in cost(kind, name, k).items():
+            free[link] = begin + time
+            end = max(end, begin + time + latency[link])
+        pending.append((kind, name, k + 1, end))
 
     for name, index, time, needs, feeds in steps_of():
         taken = plan.setdefault((name, index), [])
 
-        def open_needs():
+        def missing():
             if "all" in needs:
-                return list(pending)
-            return [i for i in pending if i[0] == "g" and i[1] in needs]
-
+                return bool(pending)
+            return any(("g", n) not in arrived for n in needs)
+
+        begun = now
         while True:
-            ready = [i for i in pending if start_of(i) <= now + 0.3 and i[3] <= now]
+            ready = [i for i in pending if i[3] <= now and start_of(i) <= now + max(1.0, 0.5 * time)]
             if ready:
-                item = min(ready, key=lambda i: (start_of(i), rank.get(i[:2], 99)))
-            elif open_needs():
-                item = min(pending, key=lambda i: (start_of(i), rank.get(i[:2], 99)))
-                now = max(now, start_of(item), item[3])
+                item = min(ready, key=lambda i: rank[i[:2]])
+            elif missing():
+                item = min(pending, key=lambda i: (max(start_of(i), i[3]), rank[i[:2]]))
+                now = max(now, item[3], start_of(item))
             else:
                 break
             taken.append(item[:3])
             issue(item, now)
+        model.append((begun, now, name, index, taken))
         now += time
         for fed in feeds:
             pending.append(("s", fed, 0, now))
-    return plan
+    return plan, model
 
 
 def norm(values):
@@ -380,8 +401,9 @@
     clips = tokens_n // CLIP_LEN
     tiles = tokens_n // TILE
     chunks = FF // CHUNK
-    bits = len(LINK) if linked else 0
+    bits = BITS if linked else 0
     lead = (slice(None),) * bits
+    base_of, stride_of = {}, {}
 
     load_x = pltpu.make_async_copy(r.tokens, r.x, r.local.at[0])
     load_cot = pltpu.make_async_copy(r.cotangent, r.dy, r.local.at[1])
@@ -391,8 +413,9 @@
     if linked:
         me, partner = place(dp, fs)
         barrier = pltpu.get_barrier_semaphore()
-        for t in range(bits):
-            pl.semaphore_signal(barrier, inc=1, device_id=partner(t), device_id_type=MESH)
+        friends = [mask for hop in (Z, XY, CORE) for mask in masks_of(hop)]
+        for mask in friends:
+            pl.semaphore_signal(barrier, inc=1, device_id=partner(mask), device_id_type=MESH)
         own = tuple(me)
 
         def share(flat, buf, rows, width, place_of):
@@ -401,53 +424,65 @@
                 buf[own + (slice(None), slice(128 * place_of(j), 128 * place_of(j) + 128))] = part
 
         per = VEC // (dp * fs)
-        start = (lax.axis_index("dp") * fs + lax.axis_index("fsdp")) * per
-        row, lane0 = start // 128, start % 128
+        lane0 = (lax.axis_index("dp") * fs + lax.axis_index("fsdp")) * per % 128
         part = r.vectors[...].astype(BF16).astype(F32)
         lane = lax.broadcasted_iota(jnp.int32, (1, 128), 1)
         first = pltpu.roll(part[:, :128], lane0, 1)
         tail = jnp.concatenate([part[:, 128:], jnp.zeros((1, 256 - per), F32)], axis=1)
         second = pltpu.roll(tail, lane0, 1)
-        r.vec[0] = jnp.zeros((VROWS, 128), F32)
-        r.vec[0, pl.ds(row, 1), :] = jnp.where(lane >= lane0, first, 0.0)
-        r.vec[0, pl.ds(row + 1, 1), :] = jnp.where(lane < lane0, first, second)
-        r.vec[0, pl.ds(row + 2, 1), :] = jnp.where(lane < lane0, second, 0.0)
+        r.vec_parts[own] = jnp.concatenate(
+            [
+                jnp.where(lane >= lane0, first, 0.0),
+                jnp.where(lane < lane0, first, second),
+                jnp.where(lane < lane0, second, 0.0),
+                jnp.zeros((5, 128), F32),
+            ],
+            axis=0,
+        )
         share(r.qkv_weight, r.wq, 16, 12, lambda j: (j % PAIRS) * 3 + j // PAIRS)
         share(r.proj_weight, r.wo, 16, 4, lambda j: j)
         share(r.up_weight, r.w1, 16, 16, lambda j: j)
         share(r.down_weight, r.w2, 64, 4, lambda j: j)
 
         jobs = {}
-        for n, (name, _, _, which) in enumerate(streams_of()):
-            order = ORDER[which]
-            gs, gr, ss, sr = r.gather_send.at[n], r.gather_recv.at[n], r.sum_send.at[n], r.sum_recv.at[n]
+        for n, (name, (hops, left, rows, width, _)) in enumerate(streams_of().items()):
+            sems = [lambda k, ref=ref, n=n: ref.at[n, k] for ref in r.sems]
             kind, number = name[0], int(name[1:]) if name[1:].isdigit() else 0
-            back = order[::-1]
+            cols = slice(number * width, number * width + width)
             if name == "vec":
-                jobs["g", name] = Sum(partner, order, r.vec, r.vec_come, gs, gr)
-                jobs["s", name] = Sum(partner, back, r.gvec, r.gvec_come, ss, sr)
-                continue
-            rows, width, base, matrix, stage, come, come0 = {
-                "q": (16, 384, 0, r.wq, r.sq, r.come, 0),
-                "o": (16, 512, 192, r.wo, r.wo, r.come, 1536),
-                "u": (16, 512, 256, r.w1, r.w1, r.come, 2048),
-                "d": (64, 256, 512, r.w2, r.w2, r.come_down, 0),
-            }[kind]
-            cols = slice(number * width, number * width + width)
-            come_cols = slice(come0 + number * width, come0 + number * width + width)
-
-            def finish(total, kind=kind, number=number, rows=rows, width=width, base=base):
-                for j in range(width // 128):
-                    col = j * PAIRS + number if kind == "q" else number * (width // 128) + j
-                    stride = {"q": 12, "o": 4, "u": 16, "d": 4}[kind]
-                    r.total[pl.ds(base + col, rows, stride=stride), :] = total[:, 128 * j : 128 * j + 128]
-
-            jobs["g", name] = Gather(me, partner, order, matrix, cols, gs, gr)
+                matrix, stage, cols, base, stride = r.vec_parts, r.gvec_parts, slice(None), 0, 0
+            elif kind == "q":
+                matrix, stage, base, stride = r.wq, r.sq, 0, 12
+            elif kind == "o":
+                matrix, stage, base, stride = r.wo, r.wo, 192, 4
+            elif kind == "u":
+                matrix, stage, base, stride = r.w1, r.w1, 256, 16
+            elif name == "dz":
+                matrix, stage, cols, base, stride = r.w2, r.down_part, slice(None), 512, 4
+            else:
+                matrix = stage = r.w2.at[number // 2, number % 2]
+                cols = slice(None)
+
+            def finish(total, name=name, kind=kind, number=number, rows=rows, width=width):
+                if name == "vec":
+                    r.total_vec[...] = total
+                elif kind == "d" and name != "dz":
+                    r.down_part[number // 2, number % 2] = total.astype(BF16)
+                else:
+                    for j in range(width // 128):
+                        col = j * PAIRS + number if kind == "q" else number * (width // 128) + j
+                        at = pl.ds(base_of[name] + col, rows, stride=stride_of[name])
+                        r.total[at, :] = total[:, 128 * j : 128 * j + 128]
+
+            if name == "vec" or name == "dz" or kind != "d":
+                base_of[name], stride_of[name] = base, stride
+            jobs["g", name] = Gather(me, partner, hops, left, matrix, cols, *sems[:2])
+            sum_left = left if name != "dz" else Z
             jobs["s", name] = Scatter(
-                me, partner, back, stage, cols, come, come_cols, ss, sr, finish
+                me, partner, hops[::-1], sum_left, stage, cols, r.come[name], *sems[2:], finish
             )
-        plan = plan_of()
-        pl.semaphore_wait(barrier, bits)
+        plan = plan_of()[0]
+        pl.semaphore_wait(barrier, len(friends))
     else:
         loads = [
             pltpu.make_async_copy(src, dst, r.local.at[3 + n])
@@ -457,7 +492,7 @@
         ]
         for load in loads:
             load.start()
-        r.vec[0] = r.vec_in[...]
+        r.vec[...] = r.vec_in[...]
         for load in loads:
             load.wait()
 
@@ -478,8 +513,7 @@
             else:
                 pl.when(index == at)(act)
 
-    vec = r.vec.at[bits]
-    gvec = r.gvec.at[0]
+    vec, gvec = r.vec, r.gvec
     gvec[...] = jnp.zeros((VROWS, 128), F32)
 
     def vector(first, count):
@@ -514,6 +548,11 @@
 
     lax.fori_loop(0, tokens_n // 256, norm_one, 0)
     exchange("affine", 0)
+    if linked:
+        vec[...] = jnp.zeros((VROWS, 128), F32)
+        for n in range(dp * fs):
+            row = n * per // 128
+            vec[row : row + 3, :] += r.vec_parts[split_bits(n) + (slice(0, 3),)]
 
     def affine_one(i, carry):
         rows = rows_of(i, 256)
@@ -661,23 +700,39 @@
 
     lax.fori_loop(0, PAIRS * clips, backward, 0)
 
-    def first_back(i, carry):
-        exchange("ln1", i)
+    def first_sums(i, carry):
+        exchange("sums", i)
         rows = rows_of(i, TILE)
         grad = dot(r.big[rows, :], whole(r.wq, slice(None)), NT)
         hat, scale = norm(r.x[rows, :].astype(F32))
         add_vector(G1, column_sum(grad * hat))
         add_vector(S1, column_sum(grad))
-        r.grad_h[rows, :] += norm_back(grad, hat, scale, vector(G1, 4))
+        r.total_out[rows, :] = grad
+        r.hat[rows, :] = hat
+        r.scale[rows, :] = jnp.broadcast_to(scale, (TILE, 128))
+        return carry
+
+    lax.fori_loop(0, tiles, first_sums, 0)
+    if linked:
+        for n in range(dp * fs):
+            row = n * per // 128
+            r.gvec_parts[split_bits(n)] = jnp.concatenate(
+                [gvec[row : row + 3, :], jnp.zeros((5, 128), F32)], axis=0
+            )
+
+    def first_back(i, carry):
+        exchange("ln1", i)
+        rows = rows_of(i, TILE)
+        r.grad_h[rows, :] += norm_back(
+            r.total_out[rows, :], r.hat[rows, :], r.scale[rows, :1], vector(G1, 4)
+        )
         return carry
 
     lax.fori_loop(0, tiles, first_back, 0)
     store_grad = pltpu.make_async_copy(r.grad_h, r.input_grad, r.local.at[3])
     store_grad.start()
     exchange("end", 0)
-    if linked:
-        r.total_vec[...] = r.gvec[bits]
-    else:
+    if not linked:
         stores = [
             pltpu.make_async_copy(src, dst, r.local.at[4 + n])
             for n, (src, dst) in enumerate(
@@ -701,11 +756,11 @@
         pl.BlockSpec(memory_space=pltpu.SMEM),
         pl.BlockSpec(memory_space=pl.ANY),
     )
-    bits = len(LINK) if linked else 0
+    bits = BITS if linked else 0
     ins = ["tokens", "cotangent", "cond_frames"]
     in_specs = [any_, any_, smem]
     outs = {"output": ((n, D), BF16, any_), "input_grad": ((n, D), F32, any_)}
-    outs["total_vec"] = ((VROWS, 128), F32, vmem)
+    outs["total_vec"] = ((8 if linked else VROWS, 128), F32, vmem)
     if linked:
         ins += ["qkv_weight", "proj_weight", "up_weight", "down_weight", "vectors"]
         in_specs += [vmem] * 5
@@ -738,32 +793,40 @@
         "wo": matrix(D, D),
         "w1": matrix(D, FF),
         "w2": matrix(FF, D),
-        "vec": pltpu.VMEM((bits + 1, VROWS, 128), F32),
-        "gvec": pltpu.VMEM((bits + 1, VROWS, 128), F32),
+        "vec": pltpu.VMEM((VROWS, 128), F32),
+        "gvec": pltpu.VMEM((VROWS, 128), F32),
         "local": pltpu.SemaphoreType.DMA((8,)),
     }
     names = ins + list(outs) + list(scratch)
     shapes = list(scratch.values())
+    come_names = []
     if linked:
-        count = len(streams_of())
-        for name in ("vec_come", "gvec_come"):
+        streams = streams_of()
+        for name in ("vec_parts", "gvec_parts"):
             names.append(name)
-            shapes.append(pltpu.VMEM((bits, VROWS, 128), F32))
+            shapes.append(pltpu.VMEM((2,) * bits + (8, 128), F32))
+        names.append("down_part")
+        shapes.append(pltpu.VMEM((2, 2, 64, D), BF16))
         for name in ("gather_send", "gather_recv", "sum_send", "sum_recv"):
             names.append(name)
-            shapes.append(pltpu.SemaphoreType.DMA((count, bits)))
-        for k in range(bits):
-            names.append(f"come{k}")
-            shapes.append(pltpu.VMEM((2,) * (bits - 1 - k) + (16, 8 * D), BF16))
-        for k in range(bits):
-            names.append(f"come_down{k}")
-            shapes.append(pltpu.VMEM((2,) * (bits - 1 - k) + (64, D), BF16))
+            shapes.append(pltpu.SemaphoreType.DMA((len(streams), 7)))
+        for name, (hops, left, rows, width, size) in streams.items():
+            held = len(left) if name != "dz" else 2
+            for k, hop in enumerate(hops[::-1]):
+                held -= len(hop)
+                come_names.append((name, f"{name}_{k}"))
+                names.append(f"{name}_{k}")
+                kind = BF16 if size == 2 else F32
+                shapes.append(pltpu.VMEM((len(masks_of(hop)),) + (2,) * held + (rows, width), kind))
 
     def body(*refs):
         table = dict(zip(names, refs))
         if linked:
-            table["come"] = [table.pop(f"come{k}") for k in range(bits)]
-            table["come_down"] = [table.pop(f"come_down{k}") for k in range(bits)]
+            table["come"] = {}
+            for name, key in come_names:
+                table["come"].setdefault(name, []).append(table.pop(key))
+            keys = ("gather_send", "gather_recv", "sum_send", "sum_recv")
+            table["sems"] = [table.pop(key) for key in keys]
         block_kernel(dp, fs, n, linked, list(table), *table.values())
 
     params = dict(vmem_limit_bytes=64 << 20)
@@ -790,56 +853,80 @@
     return (first_new, second_new, weight_new, average_new)
 
 
-def adam_kernel(dp, fs, *refs):
-    total, total_vec = refs[:2]
-    ins, outs = refs[2:22], refs[22:]
+def adam_kernel(dp, fs, linked, *refs):
+    total, total_vec, output, input_grad = refs[:4]
+    ins, outs, (output_new, input_grad_new) = refs[4:24], refs[24:44], refs[44:46]
+    held, made, passing = refs[46:66], refs[66:86], refs[86:88]
+    fetched, moved, loaded, stored = refs[88:]
+    loads = [pltpu.make_async_copy(a, b, loaded.at[n]) for n, (a, b) in enumerate(zip(ins, held))]
+    stores = [pltpu.make_async_copy(a, b, stored.at[n]) for n, (a, b) in enumerate(zip(made, outs))]
+    fetches, moves = [], []
+    for a, b, c in ((input_grad, passing[0], input_grad_new), (output, passing[1], output_new)):
+        size = a.shape[0] // 4
+        for n in range(4):
+            rows, at = pl.ds(n * size, size), len(moves)
+            fetches.append(pltpu.make_async_copy(a.at[rows, :], b.at[rows, :], fetched.at[at]))
+            moves.append(pltpu.make_async_copy(b.at[rows, :], c.at[rows, :], moved.at[at]))
+    for load in fetches + loads:
+        load.start()
+    for fetch, move in zip(fetches, moves):
+        fetch.wait()
+        move.start()
+
+    def update(m, grad, rate, decay):
+        for load in loads[4 * m : 4 * m + 4]:
+            load.wait()
+        weight, first, second, average = (ref[...] for ref in held[4 * m : 4 * m + 4])
+        new = adamw(weight, grad, first, second, average, rate, decay)
+        for ref, value in zip(made[4 * m : 4 * m + 4], new):
+            ref[...] = value
+        for store in stores[4 * m : 4 * m + 4]:
+            store.start()
+
     base = 0
     for m in range(4):
-        weight, first, second, average = ins[4 * m : 4 * m + 4]
-        size = weight.shape[0]
-        new = adamw(
-            weight[...], total[base : base + size, :], first[...], second[...], average[...],
-            RATE_MATRIX, WEIGHT_DECAY,
-        )
-        for ref, value in zip(outs[4 * m : 4 * m + 4], new):
-            ref[...] = value
+        size = held[4 * m].shape[0]
+        update(m, total[base : base + size, :], RATE_MATRIX, WEIGHT_DECAY)
         base += size
     per = VEC // (dp * fs)
     start = (lax.axis_index("dp") * fs + lax.axis_index("fsdp")) * per
-    row, lane0 = start // 128, start % 128
+    lane0 = start % 128
     lane = lax.broadcasted_iota(jnp.int32, (1, 128), 1)
     back = lax.rem(128 - lane0, 128)
+    row = 0 if linked else start // 128
     parts = [pltpu.roll(total_vec[pl.ds(row + n, 1), :], back, 1) for n in range(3)]
     keep = 128 - lane0
     grad = jnp.concatenate(
         [jnp.where(lane < keep, parts[0], parts[1]), jnp.where(lane < keep, parts[1], parts[2])], axis=1
     )[:, :per]
-    weight, first, second, average = ins[16:]
-    new = adamw(
-        weight[...], grad, first[...], second[...], average[...], RATE_VECTOR, 0.0
-    )
-    for ref, value in zip(outs[16:], new):
-        ref[...] = value
-
-
-def run_adam(dp, fs, total, total_vec, state):
+    update(4, grad, RATE_VECTOR, 0.0)
+    for copy in stores + moves:
+        copy.wait()
+
+
+def run_adam(dp, fs, linked, total, total_vec, output, input_grad, state):
     flat = [a.reshape(-1, 128) for a in state[:16]] + list(state[16:])
-    vmem = pl.BlockSpec(memory_space=pltpu.VMEM)
+    vmem, any_ = pl.BlockSpec(memory_space=pltpu.VMEM), pl.BlockSpec(memory_space=pl.ANY)
+    shapes = [jax.ShapeDtypeStruct(a.shape, F32) for a in flat]
+    shapes += [jax.ShapeDtypeStruct(a.shape, a.dtype) for a in (output, input_grad)]
     new = pl.pallas_call(
-        functools.partial(adam_kernel, dp, fs),
-        out_shape=[jax.ShapeDtypeStruct(a.shape, F32) for a in flat],
-        in_specs=[vmem] * 22,
-        out_specs=[vmem] * 20,
+        functools.partial(adam_kernel, dp, fs, linked),
+        out_shape=shapes,
+        in_specs=[vmem] * 2 + [any_] * 22,
+        out_specs=[any_] * 22,
+        scratch_shapes=[pltpu.VMEM(a.shape, F32) for a in flat] * 2
+        + [pltpu.VMEM(a.shape, a.dtype) for a in (input_grad, output)]
+        + [pltpu.SemaphoreType.DMA((n,)) for n in (8, 8, 20, 20)],
         compiler_params=pltpu.CompilerParams(vmem_limit_bytes=64 << 20),
         name="adam",
-    )(total, total_vec, *flat)
-    return [a.reshape(b.shape) for a, b in zip(new, state)]
+    )(total, total_vec, output, input_grad, *flat)
+    return list(new[20:]) + [a.reshape(b.shape) for a, b in zip(new, state)]
 
 
 def local(dp, fs, tokens, cotangent, cond_frames, *state):
     weights, firsts, seconds, averages = (state[5 * n : 5 * n + 5] for n in range(4))
     shards = dp * fs
-    linked = shards == 2 ** len(LINK) and not (dp & (dp - 1))
+    linked = shards == 2**BITS and not (dp & (dp - 1))
     if linked:
         shares = [w.reshape(-1, 128) for w in weights[:4]] + [weights[4]]
         output, input_grad, total_vec, total = run_block(
@@ -862,8 +949,7 @@
         total = jnp.concatenate([scatter(g).reshape(-1, 128) for g in grads], axis=0)
         total_vec = lax.psum(total_vec, AXES)
     order = [group[m] for m in range(5) for group in (weights, firsts, seconds, averages)]
-    new = run_adam(dp, fs, total, total_vec, order)
-    return (output, input_grad, *new)
+    return tuple(run_adam(dp, fs, linked, total, total_vec, output, input_grad, order))
 
 
 def solution(mesh):

time: 158 us -> 147 us (0.930)
  Pallas kernels: 152 us -> 146 us
  local copies, waits for them, and re-layouts: 5.22 us -> 0 us
    pallas_call x1, Pallas kernels: 149 us -> 138 us  [run_block(): pl.pallas_call(body, out_shape=[shape(s, t) for s, t, _ in outs.values()]...]
    unnamed x4 -> x0, local copies, waits for them, and re-layouts: 5.22 us -> none
    pallas_call x1, Pallas kernels: 2.95 us -> 7.91 us  [run_adam(): pl.pallas_call(functools.partial(adam_kernel, dp, fs, linked), out_shape=...]
where the time goes in v2:
time: 147 us
  Pallas kernels  146 us (99%)
    pallas_call x1, Pallas kernels, run_block(): pl.pallas_call(body, out_shape=[shape(s, t) for s, t, _ in outs.values()]...  138 us
    pallas_call x1, Pallas kernels, run_adam(): pl.pallas_call(functools.partial(adam_kernel, dp, fs, linked), out_shape=...  7.91 us

profile of v2, /device:TPU:0, one launch (start us, length us, event | category | flops | bytes accessed | tf_op | source)
XLA Modules:
  0.0 146.7 jit_solution(3068906257547800204)
XLA Ops:
  0.7 138.0 %block.1 = (bf16[2048,512]{1,0:T(8,128)(2,1)}, f32[2048,512]{1,0:T(8,128)}, f32[8,128]{1,0:T(8,128)}, f32[768,128]{1,0:T(8,128)}) custom-call(bf16[2048,512]{1,0:T(8,128)(2,1)} %refs_0_.1, bf16[2048,512]{1,0:T(8,128)(2,1)} %refs_1_.1, s32[2]{0:T(128)} %refs_2_.1, f32[192,128]{1,0:T(8,128)} %bitcast.36, f32[64,128]{1,0:T(8,128)} %bitcast.44, ...), custom_call_target="tpu_custom_call" | custom-call | tf_op jit(solution)/shard_map/block/pallas_call | solution.py:835
  138.6 7.9 %adam.1 = (f32[192,128]{1,0:T(8,128)}, f32[192,128]{1,0:T(8,128)}, f32[192,128]{1,0:T(8,128)}, f32[192,128]{1,0:T(8,128)}, f32[64,128]{1,0:T(8,128)}, /*index=5*...) custom-call(f32[768,128]{1,0:T(8,128)} %get-tuple-element.48.refs_0_, ...), custom_call_target="tpu_custom_call" | custom-call | tf_op jit(solution)/shard_map/adam/pallas_call | solution.py:912

commit v3 on v2

--- a/solution.py
+++ b/solution.py
@@ -145,6 +145,9 @@
 
     def arrived(self, k):
         source, at, come, count = self.sums[k]
+        if k + 1 < len(self.hops) and count == 1:
+            come[0] = source[at] + come[0]
+            return
         total = source[at].astype(F32)
         for slot in range(count):
             total = total + come[slot].astype(F32)
@@ -172,21 +175,22 @@
 
 
 def steps_of():
-    steps = [("norm", 0, 3.0, [], []), ("affine", 0, 0.8, ["vec"], [])]
-    steps += [("fwd", t, 2.0 + (t % 2 == 0), [f"q{t // 2}"], []) for t in range(2 * PAIRS)]
-    steps += [("mid", 0, 3.0, ["o"], [])]
+    steps = [("first", 0, 0.6, [], []), ("norm", 0, 1.5, [], []), ("affine", 0, 0.8, ["vec"], [])]
+    steps += [("fwd", t, 2.1 + (t % 2 == 0), [f"q{t // 2}"], []) for t in range(2 * PAIRS)]
+    steps += [("mid", 0, 3.1, ["o"], [])]
     for c in range(FF // CHUNK):
-        steps += [("ffa", c, 7.5, ["dz", f"d{c}", f"u{c}"], []), ("ffb", c, 2.5, [], [f"u{c}", f"d{c}"])]
-    steps += [("ln2", 0, 5.0, [], ["o"])]
+        steps += [("ffa", c, 4.4, ["dz", f"d{c}", f"u{c}"], []), ("ffb", c, 2.4, [], [f"u{c}", f"d{c}"])]
+    steps += [("ln2", 0, 5.5, [], ["o"])]
     steps += [("bwd", t, 3.5 + (t % 2), [], [f"q{t // 2}"] if t % 2 else []) for t in range(2 * PAIRS)]
     steps += [("sums", t, 1.0, [], ["vec"] if t == 3 else []) for t in range(4)]
     steps += [("ln1", t, 0.6, [], []) for t in range(4)]
+    steps += [("out", t, 1.1, [], []) for t in range(4)]
     steps += [("end", 0, 0.0, ["all"], [])]
     return steps
 
 
 def plan_of():
-    latency = {"z": 2.0, "y": 2.0, "x": 2.0, "core": 0.8}
+    latency = {"z": 2.5, "y": 2.2, "x": 2.2, "core": 0.8}
     rate = {"z": 45e3, "y": 45e3, "x": 45e3, "core": 250e3}
     free = dict.fromkeys(rate, 0.0)
     streams = streams_of()
@@ -196,7 +200,8 @@
     arrived = {}
     after = {("g", f"d{c}"): [("g", "dz")] for c in range(4)}
     after["s", "dz"] = [("s", f"d{c}") for c in range(4)]
-    pending = [("g", s, 0, 0.0) for s in streams if ("g", s) not in after]
+    early = ("vec", "q0")
+    pending = [("g", s, 0, 0.0 if s in early else 0.5) for s in streams if ("g", s) not in after]
     plan, model = {}, []
     now = 0.0
 
@@ -242,7 +247,11 @@
 
         begun = now
         while True:
-            ready = [i for i in pending if i[3] <= now and start_of(i) <= now + max(1.0, 0.5 * time)]
+            ready = [
+                i
+                for i in pending
+                if i[3] <= now and start_of(i) <= now + max(1.0, 0.5 * time)
+            ]
             if ready:
                 item = min(ready, key=lambda i: rank[i[:2]])
             elif missing():
@@ -277,10 +286,9 @@
 
 def gelu_both(pre):
     square = pre * pre
-    tanh = jnp.tanh(pre * (GELU_A + (GELU_A * GELU_B) * square))
-    half = 0.5 + 0.5 * tanh
+    half = 0.5 + 0.5 * jnp.tanh(pre * (GELU_A + (GELU_A * GELU_B) * square))
     act = pre * half
-    return act, half + act * (1.0 - tanh) * (GELU_A + (3 * GELU_A * GELU_B) * square)
+    return act, half + (act - act * half) * (2 * GELU_A + (6 * GELU_A * GELU_B) * square)
 
 
 def column_sum(values):
@@ -407,8 +415,6 @@
 
     load_x = pltpu.make_async_copy(r.tokens, r.x, r.local.at[0])
     load_cot = pltpu.make_async_copy(r.cotangent, r.dy, r.local.at[1])
-    load_x.start()
-    load_cot.start()
 
     if linked:
         me, partner = place(dp, fs)
@@ -417,6 +423,12 @@
         for mask in friends:
             pl.semaphore_signal(barrier, inc=1, device_id=partner(mask), device_id_type=MESH)
         own = tuple(me)
+        loads = {}
+        for n, name in enumerate(("vectors", "qkv_weight", "proj_weight", "up_weight", "down_weight")):
+            loads[name] = pltpu.make_async_copy(getattr(r, name), getattr(r, "my_" + name), r.local.at[3 + n])
+            loads[name].start()
+        load_x.start()
+        load_cot.start()
 
         def share(flat, buf, rows, width, place_of):
             for j in range(width):
@@ -425,7 +437,8 @@
 
         per = VEC // (dp * fs)
         lane0 = (lax.axis_index("dp") * fs + lax.axis_index("fsdp")) * per % 128
-        part = r.vectors[...].astype(BF16).astype(F32)
+        loads["vectors"].wait()
+        part = r.my_vectors[...].astype(BF16).astype(F32)
         lane = lax.broadcasted_iota(jnp.int32, (1, 128), 1)
         first = pltpu.roll(part[:, :128], lane0, 1)
         tail = jnp.concatenate([part[:, 128:], jnp.zeros((1, 256 - per), F32)], axis=1)
@@ -439,10 +452,8 @@
             ],
             axis=0,
         )
-        share(r.qkv_weight, r.wq, 16, 12, lambda j: (j % PAIRS) * 3 + j // PAIRS)
-        share(r.proj_weight, r.wo, 16, 4, lambda j: j)
-        share(r.up_weight, r.w1, 16, 16, lambda j: j)
-        share(r.down_weight, r.w2, 64, 4, lambda j: j)
+        loads["qkv_weight"].wait()
+        share(r.my_qkv_weight, r.wq, 16, 12, lambda j: (j % PAIRS) * 3 + j // PAIRS)
 
         jobs = {}
         for n, (name, (hops, left, rows, width, _)) in enumerate(streams_of().items()):
@@ -460,7 +471,7 @@
             elif name == "dz":
                 matrix, stage, cols, base, stride = r.w2, r.down_part, slice(None), 512, 4
             else:
-                matrix = stage = r.w2.at[number // 2, number % 2]
+                matrix, stage = r.w2.at[number // 2, number % 2], r.sd.at[number // 2, number % 2]
                 cols = slice(None)
 
             def finish(total, name=name, kind=kind, number=number, rows=rows, width=width):
@@ -484,6 +495,8 @@
         plan = plan_of()[0]
         pl.semaphore_wait(barrier, len(friends))
     else:
+        load_x.start()
+        load_cot.start()
         loads = [
             pltpu.make_async_copy(src, dst, r.local.at[3 + n])
             for n, (src, dst) in enumerate(
@@ -538,12 +551,21 @@
     normed_two = lambda rows: r.big.at[rows, pl.ds(1024, 512)]
     everything = pl.ds(0, tokens_n)
 
+    exchange("first", 0)
+    if linked:
+        for name, buf, rows, width in (
+            ("proj_weight", r.wo, 16, 4),
+            ("up_weight", r.w1, 16, 16),
+            ("down_weight", r.w2, 64, 4),
+        ):
+            loads[name].wait()
+            share(getattr(r, "my_" + name), buf, rows, width, lambda j: j)
     exchange("norm", 0)
     load_x.wait()
 
     def norm_one(i, carry):
         rows = rows_of(i, 256)
-        r.hat[rows, :] = norm(r.x[rows, :].astype(F32))[0]
+        r.grad_h[rows, :] = norm(r.x[rows, :].astype(F32))[0]
         return carry
 
     lax.fori_loop(0, tokens_n // 256, norm_one, 0)
@@ -556,7 +578,7 @@
 
     def affine_one(i, carry):
         rows = rows_of(i, 256)
-        r.a[rows, :] = (r.hat[rows, :] * vector(G1, 4) + vector(S1, 4)).astype(BF16)
+        r.a[rows, :] = (r.grad_h[rows, :] * vector(G1, 4) + vector(S1, 4)).astype(BF16)
         return carry
 
     lax.fori_loop(0, tokens_n // 256, affine_one, 0)
@@ -586,10 +608,10 @@
         rows = rows_of(i, TILE)
         h = r.x[rows, :].astype(F32) + dot(r.mixed[rows, :], whole(r.wo, slice(None))) + vector(BO, 4)
         hat, scale = norm(h)
-        r.hat[rows, :] = hat
+        r.hat[rows, :] = hat.astype(BF16)
         r.scale[rows, :] = jnp.broadcast_to(scale, (TILE, 128))
         normed_two(rows)[...] = (hat * vector(G2, 4) + vector(S2, 4)).astype(BF16)
-        r.total_out[rows, :] = h + vector(B2, 4)
+        r.h_low[rows, :] = (h + vector(B2, 4)).astype(BF16)
         r.grad_h[rows, :] = jnp.zeros((TILE, D), F32)
         per = CLIP_LEN // TILE
         place_in = (i % per) * TILE + lax.broadcasted_iota(jnp.int32, (TILE, 1), 0)
@@ -600,6 +622,10 @@
 
     lax.fori_loop(0, tiles, middle, 0)
 
+    def park_of(c):
+        cols = pl.ds(pl.multiple_of(c * CHUNK, CHUNK), CHUNK)
+        return pltpu.make_async_copy(act(everything), r.parked.at[:, cols], r.local.at[2])
+
     def feed(c, carry):
         exchange("ffa", c)
         cols = pl.ds(pl.multiple_of(c * CHUNK, CHUNK), CHUNK)
@@ -610,7 +636,13 @@
         def products(rows):
             return dot(normed_two(rows)[...], up), dot(r.dy[rows, :], down, NT)
 
-        ready = products(spans[0])
+        park = park_of(c)
+
+        @pl.when(c > 0)
+        def _():
+            park.wait()
+
+        ready, late = products(spans[0]), None
         bias_grad = jnp.zeros((1, CHUNK), F32)
         for i, rows in enumerate(spans):
             pre, grad_act = ready
@@ -618,46 +650,53 @@
                 ready = products(spans[i + 1])
             value, slope = gelu_both(pre + bias)
             value = value.astype(BF16)
-            grad = (slope * grad_act).astype(BF16)
-            bias_grad = bias_grad + column_sum(grad.astype(F32))
+            grad = slope * grad_act
+            bias_grad = bias_grad + column_sum(grad)
+            grad = grad.astype(BF16)
             act(rows)[...] = value
             grad_pre(rows)[...] = grad
-            r.total_out[rows, :] += dot(value, down)
-            r.grad_h[rows, :] += dot(grad, up, NT)
+            if late:
+                r.grad_h[late[0], :] += dot(late[1], up, NT)
+            late = (rows, grad)
+        r.grad_h[late[0], :] += dot(late[1], up, NT)
         for n in range(4):
             gvec[pl.ds(B1 + 4 * c + n, 1), :] = bias_grad[:, 128 * n : 128 * n + 128]
         exchange("ffb", c)
+        park.start()
         grad_up = dot(normed_two(everything)[...], grad_pre(everything)[...], TN).astype(BF16)
         grad_down = dot(act(everything)[...], r.dy[...], TN).astype(BF16)
         if linked:
             r.w1[lead + (slice(None), cols)] = grad_up.reshape((2,) * bits + (16, CHUNK))
-            r.w2[c // 2, c % 2] = grad_down.reshape((2,) * (bits - 2) + (64, D))
+            r.sd[c // 2, c % 2] = grad_down.reshape((2,) * (bits - 2) + (64, D))
         else:
             r.w1[:, cols] = grad_up
-            r.w2[rows_of(c, CHUNK), :] = grad_down
+            r.sd[rows_of(c, CHUNK), :] = grad_down
         return carry
 
     lax.fori_loop(0, chunks, feed, 0)
+    park_of(0).wait()
 
     exchange("ln2", 0)
     ri = lax.broadcasted_iota(jnp.int32, (128, 128), 0)
     ci = lax.broadcasted_iota(jnp.int32, (128, 128), 1)
     other_half = jnp.where((ri < 64) != (ci < 64), 1.0, 0.0).astype(BF16)
+    other_half = jnp.concatenate([other_half, other_half], axis=0)
     spare = lax.broadcasted_iota(jnp.int32, (TILE, 128), 1) & 63
     proj = whole(r.wo, slice(None))
-    grad_proj = jnp.zeros((D, D), F32)
-    for i in range(tiles):
-        rows = slice(i * TILE, i * TILE + TILE)
-        r.out_low[rows, :] = r.total_out[rows, :].astype(BF16)
-        grad, hat, scale = r.grad_h[rows, :], r.hat[rows, :], r.scale[rows, :1]
+
+    def norm_part(rows):
+        grad, hat, scale = r.grad_h[rows, :], r.hat[rows, :].astype(F32), r.scale[rows, :1]
         add_vector(G2, column_sum(grad * hat))
         add_vector(S2, column_sum(grad))
         grad = r.dy[rows, :].astype(F32) + norm_back(grad, hat, scale, vector(G2, 4))
         r.grad_h[rows, :] = grad
         low = grad.astype(BF16)
         add_vector(BO, column_sum(low.astype(F32)))
+        return low
+
+    def proj_part(rows, low):
         mixed = r.mixed[rows, :]
-        grad_proj = grad_proj + dot(mixed, low, TN)
+        part = dot(mixed, low, TN)
         grad_mixed = dot(low, proj, NT).astype(BF16)
         r.dy[rows, :] = grad_mixed
         product = grad_mixed.astype(F32) * mixed.astype(F32)
@@ -665,18 +704,25 @@
         rest = (product - high.astype(F32)).astype(BF16)
         for p in range(PAIRS):
             cols = slice(128 * p, 128 * p + 128)
-            row_dot = dot(high[:, cols], other_half) + dot(rest[:, cols], other_half)
+            row_dot = dot(jnp.concatenate([high[:, cols], rest[:, cols]], axis=1), other_half)
             top = row_dot.astype(BF16).astype(F32)
             r.mixed[rows, cols] = jnp.where(
                 spare == 0, -top, jnp.where(spare == 1, top - row_dot, 0.0)
             ).astype(BF16)
+        return part
+
+    spans = [slice(i * TILE, i * TILE + TILE) for i in range(tiles)]
+    grad_proj = jnp.zeros((D, D), F32)
+    low = norm_part(spans[0])
+    for i, rows in enumerate(spans):
+        after = norm_part(spans[i + 1]) if i + 1 < tiles else None
+        grad_proj = grad_proj + proj_part(rows, low)
+        low = after
     grad_proj = grad_proj.astype(BF16)
     if linked:
         r.wo[...] = grad_proj.reshape((2,) * bits + (16, D))
     else:
         r.wo[...] = grad_proj
-    store_out = pltpu.make_async_copy(r.out_low, r.output, r.local.at[2])
-    store_out.start()
 
     def backward(t, carry):
         exchange("bwd", t)
@@ -690,6 +736,9 @@
             sums = column_sum(grad.astype(F32))
             for n in range(3):
                 gvec[pl.ds(BQKV + 4 * n + pair, 1), :] = sums[:, 128 * n : 128 * n + 128]
+            hat, scale = norm(r.x[rows_of(pair, tokens_n // PAIRS), :].astype(F32))
+            r.hat[rows_of(pair, tokens_n // PAIRS), :] = hat.astype(BF16)
+            r.scale[rows_of(pair, tokens_n // PAIRS), :] = jnp.broadcast_to(scale, (tokens_n // PAIRS, 128))
             matrix = dot(r.a[...], grad, TN).astype(BF16)
             if linked:
                 r.sq[lead + (slice(None), cols)] = matrix.reshape((2,) * bits + (16, 384))
@@ -700,52 +749,53 @@
 
     lax.fori_loop(0, PAIRS * clips, backward, 0)
 
-    def first_sums(i, carry):
+    fetches = []
+    for c in range(chunks):
+        dst = r.qkv.at[:, c * CHUNK : c * CHUNK + CHUNK] if c < 3 else r.dy
+        src = r.parked.at[:, c * CHUNK : c * CHUNK + CHUNK]
+        fetches.append(pltpu.make_async_copy(src, dst, r.local.at[c]))
+        fetches[-1].start()
+    matrix = whole(r.wq, slice(None))
+    spans = [slice(i * TILE, i * TILE + TILE) for i in range(tiles)]
+    for i, rows in enumerate(spans):
         exchange("sums", i)
-        rows = rows_of(i, TILE)
-        grad = dot(r.big[rows, :], whole(r.wq, slice(None)), NT)
-        hat, scale = norm(r.x[rows, :].astype(F32))
-        add_vector(G1, column_sum(grad * hat))
+        grad = dot(r.big[rows, :], matrix, NT)
+        add_vector(G1, column_sum(grad * r.hat[rows, :].astype(F32)))
         add_vector(S1, column_sum(grad))
-        r.total_out[rows, :] = grad
-        r.hat[rows, :] = hat
-        r.scale[rows, :] = jnp.broadcast_to(scale, (TILE, 128))
-        return carry
-
-    lax.fori_loop(0, tiles, first_sums, 0)
+        r.a[rows, :] = grad.astype(BF16)
     if linked:
         for n in range(dp * fs):
             row = n * per // 128
             r.gvec_parts[split_bits(n)] = jnp.concatenate(
                 [gvec[row : row + 3, :], jnp.zeros((5, 128), F32)], axis=0
             )
-
-    def first_back(i, carry):
+    stores = []
+    for i, rows in enumerate(spans):
         exchange("ln1", i)
-        rows = rows_of(i, TILE)
-        r.grad_h[rows, :] += norm_back(
-            r.total_out[rows, :], r.hat[rows, :], r.scale[rows, :1], vector(G1, 4)
-        )
-        return carry
-
-    lax.fori_loop(0, tiles, first_back, 0)
-    store_grad = pltpu.make_async_copy(r.grad_h, r.input_grad, r.local.at[3])
-    store_grad.start()
+        grad = norm_back(r.a[rows, :].astype(F32), r.hat[rows, :].astype(F32), r.scale[rows, :1], vector(G1, 4))
+        r.lse[rows, :] = (r.grad_h[rows, :] + grad).astype(BF16)
+        stores.append(pltpu.make_async_copy(r.lse.at[rows, :], r.input_grad.at[rows, :], r.local.at[4 + i]))
+        stores[-1].start()
+
+    for fetch in fetches:
+        fetch.wait()
+    down = whole(r.w2, slice(None))
+    for i, rows in enumerate(spans):
+        exchange("out", i)
+        value = jnp.concatenate([r.qkv[rows, :], r.dy[rows, :]], axis=1)
+        r.mixed[rows, :] = (r.h_low[rows, :].astype(F32) + dot(value, down)).astype(BF16)
+        stores.append(pltpu.make_async_copy(r.mixed.at[rows, :], r.output.at[rows, :], r.local.at[8 + i]))
+        stores[-1].start()
     exchange("end", 0)
     if not linked:
-        stores = [
-            pltpu.make_async_copy(src, dst, r.local.at[4 + n])
-            for n, (src, dst) in enumerate(
-                [(r.sq, r.qkv_grad), (r.wo, r.proj_grad), (r.w1, r.up_grad), (r.w2, r.down_grad)]
-            )
-        ]
-        for store in stores:
-            store.start()
-        for store in stores:
-            store.wait()
+        for n, (src, dst) in enumerate(
+            [(r.sq, r.qkv_grad), (r.wo, r.proj_grad), (r.w1, r.up_grad), (r.sd, r.down_grad)]
+        ):
+            stores.append(pltpu.make_async_copy(src, dst, r.local.at[n]))
+            stores[-1].start()
         r.total_vec[...] = gvec[...]
-    store_out.wait()
-    store_grad.wait()
+    for store in stores:
+        store.wait()
 
 
 def run_block(dp, fs, linked, tokens, cotangent, cond_frames, weights):
@@ -759,11 +809,12 @@
     bits = BITS if linked else 0
     ins = ["tokens", "cotangent", "cond_frames"]
     in_specs = [any_, any_, smem]
-    outs = {"output": ((n, D), BF16, any_), "input_grad": ((n, D), F32, any_)}
+    outs = {"output": ((n, D), BF16, any_), "input_grad": ((n, D), BF16, any_)}
+    outs["parked"] = ((n, FF), BF16, any_)
     outs["total_vec"] = ((8 if linked else VROWS, 128), F32, vmem)
     if linked:
         ins += ["qkv_weight", "proj_weight", "up_weight", "down_weight", "vectors"]
-        in_specs += [vmem] * 5
+        in_specs += [any_] * 5
         outs["total"] = ((768, 128), F32, vmem)
         matrix = lambda rows, cols: pltpu.VMEM((2,) * bits + (rows // 2**bits, cols), BF16)
     else:
@@ -781,21 +832,21 @@
         "qkv": pltpu.VMEM((n, 3 * D), BF16),
         "mixed": pltpu.VMEM((n, D), BF16),
         "lse": pltpu.VMEM((n, D), BF16),
-        "hat": pltpu.VMEM((n, D), F32),
-        "total_out": pltpu.VMEM((n, D), F32),
+        "hat": pltpu.VMEM((n, D), BF16),
+        "h_low": pltpu.VMEM((n, D), BF16),
         "grad_h": pltpu.VMEM((n, D), F32),
         "scale": pltpu.VMEM((n, 128), F32),
         "big": pltpu.VMEM((n, 3 * D), BF16),
-        "out_low": pltpu.VMEM((n, D), BF16),
         "grad_qt": pltpu.VMEM((128, CLIP_LEN), F32),
         "wq": matrix(D, 3 * D),
         "sq": matrix(D, 3 * D),
         "wo": matrix(D, D),
         "w1": matrix(D, FF),
         "w2": matrix(FF, D),
+        "sd": matrix(FF, D),
         "vec": pltpu.VMEM((VROWS, 128), F32),
         "gvec": pltpu.VMEM((VROWS, 128), F32),
-        "local": pltpu.SemaphoreType.DMA((8,)),
+        "local": pltpu.SemaphoreType.DMA((12,)),
     }
     names = ins + list(outs) + list(scratch)
     shapes = list(scratch.values())
@@ -805,6 +856,9 @@
         for name in ("vec_parts", "gvec_parts"):
             names.append(name)
             shapes.append(pltpu.VMEM((2,) * bits + (8, 128), F32))
+        for name, held in zip(ins[3:], weights):
+            names.append("my_" + name)
+            shapes.append(pltpu.VMEM(held.shape, F32))
         names.append("down_part")
         shapes.append(pltpu.VMEM((2, 2, 64, D), BF16))
         for name in ("gather_send", "gather_recv", "sum_send", "sum_recv"):
@@ -856,21 +910,24 @@
 def adam_kernel(dp, fs, linked, *refs):
     total, total_vec, output, input_grad = refs[:4]
     ins, outs, (output_new, input_grad_new) = refs[4:24], refs[24:44], refs[44:46]
-    held, made, passing = refs[46:66], refs[66:86], refs[86:88]
-    fetched, moved, loaded, stored = refs[88:]
+    held, made = refs[46:66], refs[66:86]
+    low_grad, full_grad, out_low, fetched, moved, loaded, stored = refs[86:]
     loads = [pltpu.make_async_copy(a, b, loaded.at[n]) for n, (a, b) in enumerate(zip(ins, held))]
     stores = [pltpu.make_async_copy(a, b, stored.at[n]) for n, (a, b) in enumerate(zip(made, outs))]
     fetches, moves = [], []
-    for a, b, c in ((input_grad, passing[0], input_grad_new), (output, passing[1], output_new)):
+    for a, b, c, d in ((input_grad, low_grad, full_grad, input_grad_new), (output, out_low, out_low, output_new)):
         size = a.shape[0] // 4
         for n in range(4):
             rows, at = pl.ds(n * size, size), len(moves)
             fetches.append(pltpu.make_async_copy(a.at[rows, :], b.at[rows, :], fetched.at[at]))
-            moves.append(pltpu.make_async_copy(b.at[rows, :], c.at[rows, :], moved.at[at]))
+            moves.append(pltpu.make_async_copy(c.at[rows, :], d.at[rows, :], moved.at[at]))
     for load in fetches + loads:
         load.start()
-    for fetch, move in zip(fetches, moves):
+    for n, (fetch, move) in enumerate(zip(fetches, moves)):
         fetch.wait()
+        if n < 4:
+            rows = slice(n * size, n * size + size)
+            full_grad[rows, :] = low_grad[rows, :].astype(F32)
         move.start()
 
     def update(m, grad, rate, decay):
@@ -908,14 +965,14 @@
     flat = [a.reshape(-1, 128) for a in state[:16]] + list(state[16:])
     vmem, any_ = pl.BlockSpec(memory_space=pltpu.VMEM), pl.BlockSpec(memory_space=pl.ANY)
     shapes = [jax.ShapeDtypeStruct(a.shape, F32) for a in flat]
-    shapes += [jax.ShapeDtypeStruct(a.shape, a.dtype) for a in (output, input_grad)]
+    shapes += [jax.ShapeDtypeStruct(output.shape, BF16), jax.ShapeDtypeStruct(output.shape, F32)]
     new = pl.pallas_call(
         functools.partial(adam_kernel, dp, fs, linked),
         out_shape=shapes,
         in_specs=[vmem] * 2 + [any_] * 22,
         out_specs=[any_] * 22,
         scratch_shapes=[pltpu.VMEM(a.shape, F32) for a in flat] * 2
-        + [pltpu.VMEM(a.shape, a.dtype) for a in (input_grad, output)]
+        + [pltpu.VMEM(output.shape, t) for t in (BF16, F32, BF16)]
         + [pltpu.SemaphoreType.DMA((n,)) for n in (8, 8, 20, 20)],
         compiler_params=pltpu.CompilerParams(vmem_limit_bytes=64 << 20),
         name="adam",
@@ -929,7 +986,7 @@
     linked = shards == 2**BITS and not (dp & (dp - 1))
     if linked:
         shares = [w.reshape(-1, 128) for w in weights[:4]] + [weights[4]]
-        output, input_grad, total_vec, total = run_block(
+        output, input_grad, _, total_vec, total = run_block(
             dp, fs, True, tokens, cotangent, cond_frames, shares
         )
     else:
@@ -939,7 +996,7 @@
         qkv = gathered[0].reshape(D, 3, PAIRS, 128).swapaxes(1, 2).reshape(D, 3 * D)
         vec = jnp.pad(gathered[4].astype(F32).reshape(-1, 128), ((0, VROWS - VEC // 128), (0, 0)))
         mats = [qkv] + [g.reshape(-1, c) for g, c in zip(gathered[1:4], (D, FF, D))] + [vec]
-        output, input_grad, total_vec, *grads = run_block(
+        output, input_grad, _, total_vec, *grads = run_block(
             dp, fs, False, tokens, cotangent, cond_frames, mats
         )
         grads[0] = grads[0].reshape(D, PAIRS, 3, 128).swapaxes(1, 2).reshape(D, 3 * D)

time: 147 us -> 139 us (0.946)
  Pallas kernels: 146 us -> 138 us
    pallas_call x1, Pallas kernels: 138 us -> 132 us  [run_block(): pl.pallas_call(body, out_shape=[shape(s, t) for s, t, _ in outs.values()]...]
    pallas_call x1, Pallas kernels: 7.91 us -> 6.33 us  [run_adam(): pl.pallas_call(functools.partial(adam_kernel, dp, fs, linked), out_shape=...]
where the time goes in v3:
time: 139 us
  Pallas kernels  138 us (99%)
    pallas_call x1, Pallas kernels, run_block(): pl.pallas_call(body, out_shape=[shape(s, t) for s, t, _ in outs.values()]...  132 us
    pallas_call x1, Pallas kernels, run_adam(): pl.pallas_call(functools.partial(adam_kernel, dp, fs, linked), out_shape=...  6.33 us

profile of v3, /device:TPU:0, one launch (start us, length us, event | category | flops | bytes accessed | tf_op | source)
XLA Modules:
  0.0 139.1 jit_solution(2442392181067656823)
XLA Ops:
  0.7 131.9 %block.1 = (bf16[2048,512]{1,0:T(8,128)(2,1)}, bf16[2048,512]{1,0:T(8,128)(2,1)}, bf16[2048,2048]{1,0:T(8,128)(2,1)}, f32[8,128]{1,0:T(8,128)}, f32[768,128]{1,0:T(8,128)}) custom-call(bf16[2048,512]{1,0:T(8,128)(2,1)} %refs_0_.1, bf16[2048,512]{1,0:T(8,128)(2,1)} %refs_1_.1, s32[2]{0:T(128)} %refs_2_.1, f32[192,128]{1,0:T(8,128)} %bitcast.36, ...), custom_call_target="tpu_custom_call" | custom-call | tf_op jit(solution)/shard_map/block/pallas_call | solution.py:889
  132.6 6.3 %adam.1 = (f32[192,128]{1,0:T(8,128)}, f32[192,128]{1,0:T(8,128)}, f32[192,128]{1,0:T(8,128)}, f32[192,128]{1,0:T(8,128)}, f32[64,128]{1,0:T(8,128)}, /*index=5*...) custom-call(f32[768,128]{1,0:T(8,128)} %get-tuple-element.48.refs_0_, ...), custom_call_target="tpu_custom_call" | custom-call | tf_op jit(solution)/shard_map/adam/pallas_call | solution.py:969

commit v4 on v3

--- a/solution.py
+++ b/solution.py
@@ -162,7 +162,7 @@
     every = (0, 1, 2, 3, 4)
     streams = {"vec": ((Z, XY, CORE), every, 8, 128, 4)}
     for p in range(PAIRS):
-        hops = (Z, XY, CORE) if p in (0, PAIRS - 1) else (first, second)[p % 2]
+        hops = (Z, XY, CORE) if p in (0, 1, PAIRS - 1) else (first, second)[p % 2]
         streams[f"q{p}"] = (hops, every, 16, 384, 2)
     streams["o"] = (first, every, 16, 512, 2)
     streams["u0"] = (second, every, 16, 512, 2)
@@ -182,7 +182,7 @@
         steps += [("ffa", c, 4.4, ["dz", f"d{c}", f"u{c}"], []), ("ffb", c, 2.4, [], [f"u{c}", f"d{c}"])]
     steps += [("ln2", 0, 5.5, [], ["o"])]
     steps += [("bwd", t, 3.5 + (t % 2), [], [f"q{t // 2}"] if t % 2 else []) for t in range(2 * PAIRS)]
-    steps += [("sums", t, 1.0, [], ["vec"] if t == 3 else []) for t in range(4)]
+    steps += [("sums", t, 1.2, [], ["vec"] if t == 3 else []) for t in range(4)]
     steps += [("ln1", t, 0.6, [], []) for t in range(4)]
     steps += [("out", t, 1.1, [], []) for t in range(4)]
     steps += [("end", 0, 0.0, ["all"], [])]
@@ -569,6 +569,18 @@
         return carry
 
     lax.fori_loop(0, tokens_n // 256, norm_one, 0)
+    load_cot.wait()
+
+    def mask_one(i, carry):
+        rows = rows_of(i, 256)
+        per = CLIP_LEN // 256
+        place_in = (i % per) * 256 + lax.broadcasted_iota(jnp.int32, (256, 1), 0)
+        dy = jnp.where(place_in >= r.cond_frames[i // per] * FRAME_TOK, r.dy[rows, :].astype(F32), 0.0)
+        add_vector(B2, column_sum(dy))
+        r.dy[rows, :] = dy.astype(BF16)
+        return carry
+
+    lax.fori_loop(0, tokens_n // 256, mask_one, 0)
     exchange("affine", 0)
     if linked:
         vec[...] = jnp.zeros((VROWS, 128), F32)
@@ -602,7 +614,6 @@
     lax.fori_loop(0, PAIRS * clips, forward, 0)
 
     exchange("mid", 0)
-    load_cot.wait()
 
     def middle(i, carry):
         rows = rows_of(i, TILE)
@@ -613,11 +624,6 @@
         normed_two(rows)[...] = (hat * vector(G2, 4) + vector(S2, 4)).astype(BF16)
         r.h_low[rows, :] = (h + vector(B2, 4)).astype(BF16)
         r.grad_h[rows, :] = jnp.zeros((TILE, D), F32)
-        per = CLIP_LEN // TILE
-        place_in = (i % per) * TILE + lax.broadcasted_iota(jnp.int32, (TILE, 1), 0)
-        dy = jnp.where(place_in >= r.cond_frames[i // per] * FRAME_TOK, r.dy[rows, :].astype(F32), 0.0)
-        add_vector(B2, column_sum(dy))
-        r.dy[rows, :] = dy.astype(BF16)
         return carry
 
     lax.fori_loop(0, tiles, middle, 0)
@@ -736,9 +742,6 @@
             sums = column_sum(grad.astype(F32))
             for n in range(3):
                 gvec[pl.ds(BQKV + 4 * n + pair, 1), :] = sums[:, 128 * n : 128 * n + 128]
-            hat, scale = norm(r.x[rows_of(pair, tokens_n // PAIRS), :].astype(F32))
-            r.hat[rows_of(pair, tokens_n // PAIRS), :] = hat.astype(BF16)
-            r.scale[rows_of(pair, tokens_n // PAIRS), :] = jnp.broadcast_to(scale, (tokens_n // PAIRS, 128))
             matrix = dot(r.a[...], grad, TN).astype(BF16)
             if linked:
                 r.sq[lead + (slice(None), cols)] = matrix.reshape((2,) * bits + (16, 384))
@@ -760,7 +763,10 @@
     for i, rows in enumerate(spans):
         exchange("sums", i)
         grad = dot(r.big[rows, :], matrix, NT)
-        add_vector(G1, column_sum(grad * r.hat[rows, :].astype(F32)))
+        hat, scale = norm(r.x[rows, :].astype(F32))
+        r.hat[rows, :] = hat.astype(BF16)
+        r.scale[rows, :] = jnp.broadcast_to(scale, (TILE, 128))
+        add_vector(G1, column_sum(grad * hat))
         add_vector(S1, column_sum(grad))
         r.a[rows, :] = grad.astype(BF16)
     if linked:

time: 139 us -> 137 us (0.986)
  Pallas kernels: 138 us -> 136 us
    pallas_call x1, Pallas kernels: 132 us -> 129 us  [run_block(): pl.pallas_call(body, out_shape=[shape(s, t) for s, t, _ in outs.values()]...]
where the time goes in v4:
time: 137 us
  Pallas kernels  136 us (99%)
    pallas_call x1, Pallas kernels, run_block(): pl.pallas_call(body, out_shape=[shape(s, t) for s, t, _ in outs.values()]...  129 us
    pallas_call x1, Pallas kernels, run_adam(): pl.pallas_call(functools.partial(adam_kernel, dp, fs, linked), out_shape=...  6.33 us

profile of v4, /device:TPU:0, one launch (start us, length us, event | category | flops | bytes accessed | tf_op | source)
XLA Modules:
  0.0 136.6 jit_solution(9115155610975837140)
XLA Ops:
  0.7 129.4 %block.1 = (bf16[2048,512]{1,0:T(8,128)(2,1)}, bf16[2048,512]{1,0:T(8,128)(2,1)}, bf16[2048,2048]{1,0:T(8,128)(2,1)}, f32[8,128]{1,0:T(8,128)}, f32[768,128]{1,0:T(8,128)}) custom-call(bf16[2048,512]{1,0:T(8,128)(2,1)} %refs_0_.1, bf16[2048,512]{1,0:T(8,128)(2,1)} %refs_1_.1, s32[2]{0:T(128)} %refs_2_.1, f32[192,128]{1,0:T(8,128)} %bitcast.36, ...), custom_call_target="tpu_custom_call" | custom-call | tf_op jit(solution)/shard_map/block/pallas_call | solution.py:895
  130.1 6.3 %adam.1 = (f32[192,128]{1,0:T(8,128)}, f32[192,128]{1,0:T(8,128)}, f32[192,128]{1,0:T(8,128)}, f32[192,128]{1,0:T(8,128)}, f32[64,128]{1,0:T(8,128)}, /*index=5*...) custom-call(f32[768,128]{1,0:T(8,128)} %get-tuple-element.48.refs_0_, ...), custom_call_target="tpu_custom_call" | custom-call | tf_op jit(solution)/shard_map/adam/pallas_call | solution.py:975

commit v5 on v4

--- a/solution.py
+++ b/solution.py
@@ -164,7 +164,7 @@
     for p in range(PAIRS):
         hops = (Z, XY, CORE) if p in (0, 1, PAIRS - 1) else (first, second)[p % 2]
         streams[f"q{p}"] = (hops, every, 16, 384, 2)
-    streams["o"] = (first, every, 16, 512, 2)
+    streams["o"] = ((Z, XY, CORE), every, 16, 512, 2)
     streams["u0"] = (second, every, 16, 512, 2)
     streams["dz"] = ((Z,), every, 64, 512, 2)
     streams["d0"] = (first[1:], every[2:], 64, 512, 2)

time: 137 us -> 137 us (level)
  no operation moved by 1% of the time
where the time goes in v5:
time: 137 us
  Pallas kernels  136 us (99%)
    pallas_call x1, Pallas kernels, run_block(): pl.pallas_call(body, out_shape=[shape(s, t) for s, t, _ in outs.values()]...  129 us
    pallas_call x1, Pallas kernels, run_adam(): pl.pallas_call(functools.partial(adam_kernel, dp, fs, linked), out_shape=...  6.33 us

profile of v5, /device:TPU:0, one launch (start us, length us, event | category | flops | bytes accessed | tf_op | source)
XLA Modules:
  0.0 136.6 jit_solution(4766906203590662800)
XLA Ops:
  0.7 129.4 %block.1 = (bf16[2048,512]{1,0:T(8,128)(2,1)}, bf16[2048,512]{1,0:T(8,128)(2,1)}, bf16[2048,2048]{1,0:T(8,128)(2,1)}, f32[8,128]{1,0:T(8,128)}, f32[768,128]{1,0:T(8,128)}) custom-call(bf16[2048,512]{1,0:T(8,128)(2,1)} %refs_0_.1, bf16[2048,512]{1,0:T(8,128)(2,1)} %refs_1_.1, s32[2]{0:T(128)} %refs_2_.1, f32[192,128]{1,0:T(8,128)} %bitcast.36, ...), custom_call_target="tpu_custom_call" | custom-call | tf_op jit(solution)/shard_map/block/pallas_call | solution.py:895
  130.1 6.3 %adam.1 = (f32[192,128]{1,0:T(8,128)}, f32[192,128]{1,0:T(8,128)}, f32[192,128]{1,0:T(8,128)}, f32[192,128]{1,0:T(8,128)}, f32[64,128]{1,0:T(8,128)}, /*index=5*...) custom-call(f32[768,128]{1,0:T(8,128)} %get-tuple-element.48.refs_0_, ...), custom_call_target="tpu_custom_call" | custom-call | tf_op jit(solution)/shard_map/adam/pallas_call | solution.py:975
